TPU v7x, 512 devices: a whole 4x4x16 slice. The times are simulated.
512 devices in a mesh: req: 32 (over y, z_hi, x), patch: 16 (over z_lo, core).
Axes of the slice: x: 4, y: 4, z: 16 (z_hi: 2, z_lo: 8; z = z_hi * 8 + z_lo), core: 2. Of those that a mesh axis runs over, the one named last changes fastest.
Arguments:
- image_queries: bfloat16 [32, 512, 1152], P('req', 'patch'), may hold values from -256 to 256
- cross_queries: bfloat16 [32, 512, 1152], P('req', 'patch'), may hold values from -256 to 256
- fresh_kv: bfloat16 [32, 512, 2304], P('req', 'patch'), may hold values from -6 to 6
- stale_kv: bfloat16 [32, 512, 2304], P('req', 'patch'), may hold values from -6 to 6
- prompt_states: bfloat16 [32, 300, 4096], P('req', None, 'patch'), may hold values from -6 to 6
- caption_weight: bfloat16 [4096, 1152], P('patch'), may hold values from -0.09375 to 0.09375
- cross_kv_weight: bfloat16 [1152, 2304], P(None, 'patch'), may hold values from -0.1875 to 0.1875
- prompt_lengths: int32 [32], replicated, may hold values from 20 to 300, as said below
- prompt_route: int32 [32], replicated, may hold values from 0 to 31, as said below
Outputs:
- self_out: float32 [32, 512, 1152], P('req', 'patch')
- cross_out: float32 [32, 512, 1152], P('req', 'patch')
Inputs may be any that keep to these rules, and one draw needn't show every extreme that they name: `prompt_lengths`: every prompt has at least 20 and at most 300 live tokens; some prompt has exactly 300. `prompt_route`: each prompt is used by exactly one request.
All inputs are finite; a program needn't handle non-finite values.
Results may differ from a plain program's by a relative error of at most 0.012.
The roundings to bfloat16 on the way count: a program that leaves them out, or rounds other values in their place, can miss the bound.
Values may be sent and summed in bfloat16 or wider, within the bound.
A program may use at most 64 MiB of HBM per device.

v0:
```python
import jax
import jax.numpy as jnp
from jax import lax
from jax.sharding import PartitionSpec as P

HEADS = 16
HD = 72


masked_score = -1e30


def empty_carry(row_count, head_count):
    return (
        jnp.full((row_count, head_count), masked_score, jnp.float32),
        jnp.zeros((row_count, head_count), jnp.float32),
        jnp.zeros((row_count, head_count, HD), jnp.float32),
    )


def fold_keys(carried, queries, key_rows, values, visible):
    highest, weight_sum, blended = carried
    scores = jnp.einsum(
        "qhd,khd->qhk", queries, key_rows, preferred_element_type=jnp.float32
    ) * HD ** (-0.5)
    scores = jnp.where(visible[None, None, :], scores, masked_score)
    new_high = jnp.maximum(highest, jnp.max(scores, axis=-1))
    shrink = jnp.exp(highest - new_high)
    weights = jnp.exp(scores - new_high[..., None])
    weight_sum = weight_sum * shrink + jnp.sum(weights, axis=-1)
    blended = blended * shrink[..., None] + jnp.einsum(
        "qhk,khd->qhd", weights.astype(jnp.bfloat16), values, preferred_element_type=jnp.float32
    )
    return (new_high, weight_sum, blended)


def shards(
    image_queries,
    cross_queries,
    fresh_kv,
    stale_kv,
    prompt_states,
    caption_weight,
    cross_kv_weight,
    prompt_lengths,
    prompt_route,
):
    tok_rows = image_queries.shape[1]
    width = image_queries.shape[2]
    own_start = lax.axis_index("patch") * tok_rows
    source = prompt_route[lax.axis_index("req")]
    all_prompts = lax.all_gather(prompt_states, "req", axis=0, tiled=True)
    chosen = lax.dynamic_index_in_dim(all_prompts, source, 0, keepdims=False)
    partial_sum = jnp.dot(chosen, caption_weight, preferred_element_type=jnp.float32)
    summed = lax.psum(partial_sum, "patch")
    caption = jax.nn.gelu(summed, approximate=True).astype(jnp.bfloat16)
    local_heads = jnp.dot(caption, cross_kv_weight, preferred_element_type=jnp.float32).astype(
        jnp.bfloat16
    )
    head_states = lax.all_gather(local_heads, "patch", axis=1, tiled=True)
    prompt_rows = head_states.shape[0]
    head_states = head_states.reshape(prompt_rows, HEADS, 2, HD)
    length = prompt_lengths[source]
    prompt_visible = jnp.arange(prompt_rows, dtype=jnp.int32) < length
    cross_rows = cross_queries[0].reshape(tok_rows, HEADS, HD)
    cross_high, cross_sum, cross_blend = fold_keys(
        empty_carry(tok_rows, HEADS),
        cross_rows,
        head_states[:, :, 0],
        head_states[:, :, 1],
        prompt_visible,
    )
    cross_out = (cross_blend / cross_sum[..., None]).reshape(1, tok_rows, width)
    queries = image_queries[0].reshape(tok_rows, HEADS, HD)
    fresh_rows = fresh_kv[0].reshape(tok_rows, 2, HEADS, HD)
    own_part = fold_keys(
        empty_carry(tok_rows, HEADS),
        queries,
        fresh_rows[:, 0],
        fresh_rows[:, 1],
        jnp.ones((tok_rows,), dtype=bool),
    )
    carried = own_part
    rows = lax.all_gather(stale_kv, "patch", axis=1, tiled=True).reshape(-1, 2, HEADS, HD)
    block_len = 512
    positions = jnp.arange(block_len, dtype=jnp.int32)
    visible = (positions < own_start) | (positions >= own_start + tok_rows)
    carried = fold_keys(carried, queries, rows[:, 0], rows[:, 1], visible)
    final_high, final_sum, final_blend = carried
    self_out = (final_blend / final_sum[..., None]).reshape(1, tok_rows, width)
    return (self_out, cross_out)


def solution(mesh):
    in_specs = (
        P("req", "patch", None),
        P("req", "patch", None),
        P("req", "patch", None),
        P("req", "patch", None),
        P("req", None, "patch"),
        P("patch", None),
        P(None, "patch"),
        P(),
        P(),
    )
    out_specs = (P("req", "patch", None), P("req", "patch", None))
    return jax.shard_map(shards, mesh=mesh, in_specs=in_specs, out_specs=out_specs, check_vma=False)
```

profile of v0, /device:TPU:1, one launch (start us, length us, event | category | flops | bytes accessed | tf_op | source)
XLA Modules:
  0.0 615.0 jit_solution(11881572958913109493)
XLA Ops:
  7.2 0.0 copy-start
  7.2 0.0 all-gather.6.cloned.1.call-start
  7.2 0.7 all-gather.6.cloned.1.call-update
  7.9 0.0 all-reduce.2.cloned.1.call-start
  8.0 1.2 dynamic_slice.10
  11.2 0.0 copy-start.6
  11.2 188.5 %all-gather.6.cloned.1.call-done = bf16[32,300,256]{2,1,0:T(8,128)(2,1)} async-done(((bf16[1,300,256]{2,1,0:T(8,128)(2,1)}), bf16[32,300,256]{2,1,0:T(8,128)(2,1)}) %all-gather.6.cloned.1.call-update) | async-done | bytes 4915216 | tf_op jit(solution)/shard_map/all_gather | solution.py:52
  199.7 0.0 copy-done
  199.7 2.4 fusion.32
  202.1 0.0 all-reduce.2.cloned.1.call-update
  202.1 0.0 all-gather.4.cloned.1.call-start
  202.1 0.7 all-gather.4.cloned.1.call-update
  202.8 0.0 copy-start.7
  202.8 0.0 copy-start.3
  202.9 0.0 copy-start.4
  202.9 0.0 copy-start.1
  202.9 0.0 all-gather.8.cloned.1.call-start
  202.9 195.8 %all-reduce.2.cloned.1.call-done = f32[300,1152]{1,0:T(8,128)} async-done(((f32[300,1152]{1,0:T(8,128)}), f32[300,1152]{1,0:T(8,128)}) %all-reduce.2.cloned.1.call-update) | async-done | bytes 1382416 | tf_op jit(solution)/shard_map/psum | solution.py:55
  398.7 0.0 copy-done.6
  398.7 2.6 convolution_convert_fusion
  401.4 0.0 all-gather.8.cloned.1.call-update
  401.4 0.0 copy-done.7
  401.4 0.6 dynamic_slice.11
  402.0 0.0 copy-done.3
  402.0 0.2 reshape_squeeze.11
  402.2 0.0 copy-done.4
  402.3 0.2 reshape_squeeze.10
  402.5 0.0 copy-done.1
  402.5 0.5 reshape_squeeze.9
  403.0 0.7 iota_compare_fusion
  403.7 0.7 fusion.48
  404.4 0.2 fusion.49
  404.6 97.6 %all-gather.4.cloned.1.call-done = bf16[1,512,2304]{2,1,0:T(8,128)(2,1)} async-done(((bf16[1,32,2304]{2,1,0:T(8,128)(2,1)}), bf16[1,512,2304]{2,1,0:T(8,128)(2,1)}) %all-gather.4.cloned.1.call-update) | async-done | bytes 2359312 | tf_op jit(solution)/shard_map/all_gather | solution.py:84
  502.2 2.8 copy.33
  505.0 0.4 fusion.50
  505.4 0.1 fusion.30
  505.5 0.4 fusion.21
  505.8 0.0 copy-start.2
  505.9 0.5 fusion.20
  506.4 0.4 copy-done.2
  506.8 0.4 fusion.17
  507.1 0.2 copy.35
  507.3 0.8 reshape.71
  508.1 96.9 %all-gather.8.cloned.1.call-done = bf16[300,2304]{0,1:T(8,128)(2,1)} async-done(((bf16[300,144]{0,1:T(8,128)(2,1)}), bf16[300,2304]{0,1:T(8,128)(2,1)}) %all-gather.8.cloned.1.call-update) | async-done | bytes 1382416 | tf_op jit(solution)/shard_map/all_gather | solution.py:60
  605.0 0.0 copy-start.5
  605.0 1.7 fusion.51
  606.7 0.3 fusion.24
  607.0 0.0 copy-done.5
  607.1 0.5 fusion.19
  607.5 0.2 copy.39
  607.7 0.8 reshape.73
  (5 shorter events, 0.1 us)
Async XLA Ops:
  7.2 192.5 %copy-start = (bf16[256,1152]{1,0:T(8,128)(2,1)S(1)}, bf16[256,1152]{1,0:T(8,128)(2,1)}, u32[]{:S(2)}) copy-start(bf16[256,1152]{1,0:T(8,128)(2,1)} %param.14) | copy-start | bytes 1769476
  7.2 192.5 %all-gather.6.cloned.1.call-start = ((), (), s32[]{:S(2)}) async-start(), calls=%async_computation.1 | async-start | bytes 5136384 | tf_op jit(solution)/shard_map/all_gather | solution.py:52
  7.9 390.8 %all-reduce.2.cloned.1.call-start = ((), (), s32[]{:S(2)}) async-start(), calls=%async_computation.2 | async-start | bytes 2801664 | tf_op jit(solution)/shard_map/psum | solution.py:55
  11.2 387.6 %copy-start.6 = (bf16[1152,144]{0,1:T(8,128)(2,1)S(1)}, bf16[1152,144]{0,1:T(8,128)(2,1)}, u32[]{:S(2)}) copy-start(bf16[1152,144]{0,1:T(8,128)(2,1)} %param.15) | copy-start | bytes 995332
  202.1 300.1 %all-gather.4.cloned.1.call-start = ((), (), s32[]{:S(2)}) async-start(), calls=%async_computation | async-start | bytes 2506752 | tf_op jit(solution)/shard_map/all_gather | solution.py:84
  202.8 198.6 %copy-start.7 = (s32[32]{0:T(128)S(1)}, s32[32]{0:T(128)}, u32[]{:S(2)}) copy-start(s32[32]{0:T(128)} %param.16) | copy-start | bytes 388
  202.8 199.2 %copy-start.3 = (bf16[1,32,1152]{2,1,0:T(8,128)(2,1)S(1)}, bf16[1,32,1152]{2,1,0:T(8,128)(2,1)}, u32[]{:S(2)}) copy-start(bf16[1,32,1152]{2,1,0:T(8,128)(2,1)} %param.10) | copy-start | bytes 221188
  202.9 199.4 %copy-start.4 = (bf16[1,32,1152]{2,1,0:T(8,128)(2,1)S(1)}, bf16[1,32,1152]{2,1,0:T(8,128)(2,1)}, u32[]{:S(2)}) copy-start(bf16[1,32,1152]{2,1,0:T(8,128)(2,1)} %param.9) | copy-start | bytes 221188
  202.9 199.6 %copy-start.1 = (bf16[1,32,2304]{2,1,0:T(8,128)(2,1)S(1)}, bf16[1,32,2304]{2,1,0:T(8,128)(2,1)}, u32[]{:S(2)}) copy-start(bf16[1,32,2304]{2,1,0:T(8,128)(2,1)} %param.11) | copy-start | bytes 442372
  202.9 402.2 %all-gather.8.cloned.1.call-start = ((), (), s32[]{:S(2)}) async-start(), calls=%async_computation.3 | async-start | bytes 1880064 | tf_op jit(solution)/shard_map/all_gather | solution.py:60
  505.8 0.9 copy-start.2
  605.0 2.0 copy-start.5
Sparse Core Ops, SparseCore 0:
  12.3 187.3 all-gather.5
  202.6 196.0 all-reduce.1
  400.8 101.3 all-gather.3
  504.1 100.8 all-gather.7
where the time goes:
time: 615 us
  waiting for transfers between devices  580 us (94%)
  between operations  15.9 us (3%)
  local copies, waits for them, and re-layouts  8.65 us (1%)
  matrix products  8.64 us (1%)
    psum x1, waiting for transfers between devices, shards(): summed = lax.psum(partial_sum, 'patch')  196 us
    all_gather x1, waiting for transfers between devices, shards(): all_prompts = lax.all_gather(prompt_states, 'req', axis=0, tiled=True)  188 us
    all_gather x1, waiting for transfers between devices, shards(): lax.all_gather(stale_kv, 'patch', axis=1, tiled=True)  97.6 us
    all_gather x1, waiting for transfers between devices, shards(): head_states = lax.all_gather(local_heads, 'patch', axis=1, tiled=True)  96.9 us
  transfers between devices with their start and end apart: 4, of which 4 were waited for; matrix products, arithmetic and copies ran while one was open for 2% of the time, Pallas kernels for 0%

commit v1 on v0

v1 whole, which is shorter than its diff:
```python
import functools

import jax
import jax.numpy as jnp
from jax import lax
from jax.experimental import pallas as pl
from jax.experimental.pallas import tpu as pltpu
from jax.sharding import PartitionSpec as P

HEADS = 16
HD = 72
LANES = 128
TILE = 16
TILES = 11
LINE = 8
CUTS = ((0, 6), (6, 5))
masked_score = -1e30
MESH = pl.DeviceIdType.MESH


def kernel(
    dims,
    route_ref,
    lengths_ref,
    prompt_ref,
    caption_w_ref,
    kv_w_ref,
    image_q_ref,
    cross_q_ref,
    fresh_ref,
    stale_ref,
    self_out_ref,
    cross_out_ref,
    part,
    sib_part,
    from_low,
    from_high,
    routed,
    y_send,
    y_recv,
    caption,
    cq_send,
    cq_recv,
    sf_send,
    sf_recv,
    so_send,
    so_recv,
    co_send,
    co_recv,
    sib_sems,
    low_sems,
    high_sems,
    h_sems,
    x_sems,
    y_sems,
    up_sems,
    down_sems,
    gather_recv,
    twin_sems,
    cq_sems,
    sf_sems,
    so_sems,
    co_sems,
):
    n_y, n_h, n_x = dims
    me_r = lax.axis_index("req")
    me_p = lax.axis_index("patch")
    y = me_r // (n_h * n_x)
    h = (me_r // n_x) % n_h
    x = me_r % n_x
    z = me_p // 2
    c = me_p % 2
    u = z + h * (LINE - 1 - 2 * z)

    def on_line(pos, core):
        return 2 * (pos + h * (LINE - 1 - 2 * pos)) + core

    def patch_peer(i):
        return {"patch": (me_p + i) % (2 * LINE)}

    twin = {"patch": 2 * z + 1 - c}
    upper = {"patch": on_line(jnp.minimum(u + 1, LINE - 1), c)}
    lower = {"patch": on_line(jnp.maximum(u - 1, 0), c)}
    half_peer = {"req": me_r + n_x * (1 - 2 * h), "patch": 2 * (LINE - 1 - z) + c}

    def x_peer(i):
        return {"req": me_r - x + (x + i) % n_x}

    def y_peer(i):
        return {"req": ((y + i) % n_y) * (n_h * n_x) + h * n_x + x}

    def copy(src, dst, send, recv, device):
        return pltpu.make_async_remote_copy(
            src_ref=src, dst_ref=dst, send_sem=send, recv_sem=recv, device_id=device, device_id_type=MESH
        )

    barrier = pltpu.get_barrier_semaphore()
    greeted = 0
    for device in (
        [patch_peer(i) for i in range(1, 2 * LINE)]
        + [half_peer]
        + [x_peer(i) for i in range(1, n_x)]
        + [y_peer(i) for i in range(1, n_y)]
    ):
        pl.semaphore_signal(barrier, inc=1, device_id=device, device_id_type=MESH)
        greeted += 1
    pl.semaphore_wait(barrier, greeted)

    prompt = prompt_ref[0]
    rows = prompt.shape[0]
    row_tiles = -(-rows // TILE)
    prompt = jnp.concatenate(
        [prompt, jnp.zeros((row_tiles * TILE - rows, prompt.shape[1]), prompt.dtype)], axis=0
    )
    width = caption_w_ref.shape[1]
    col_tiles = width // LANES

    def place(i, j):
        piece, at = divmod(i * col_tiles + j, TILES)
        return piece // LINE, piece % LINE, at

    group = 3
    for j0 in range(0, col_tiles, group):
        block = jnp.dot(
            prompt, caption_w_ref[:, j0 * LANES : (j0 + group) * LANES], preferred_element_type=jnp.float32
        )
        for i in range(row_tiles):
            for j in range(group):
                part[place(i, j0 + j)] = block[i * TILE : (i + 1) * TILE, j * LANES : (j + 1) * LANES]
    for t in range(row_tiles * col_tiles, 2 * LINE * TILES):
        part[t // (LINE * TILES), (t // TILES) % LINE, t % TILES] = jnp.zeros((TILE, LANES), jnp.float32)

    to_twin = copy(part.at[1 - c], sib_part, sib_sems.at[0], sib_sems.at[1], twin)
    to_twin.start()

    tok = image_q_ref.shape[1]
    pad_c = jnp.zeros((tok, LANES - HD), jnp.bfloat16)
    pad_s = jnp.zeros((tok, 3 * LANES - 5 * HD), jnp.bfloat16)
    for n in range(HEADS):
        a, b = n * HD, (n + 1) * HD
        cq_send[n] = jnp.concatenate([cross_q_ref[0, :, a:b], pad_c], axis=1)
        sf_send[n] = jnp.concatenate(
            [
                image_q_ref[0, :, a:b],
                stale_ref[0, :, a:b],
                stale_ref[0, :, width + a : width + b],
                fresh_ref[0, :, a:b],
                fresh_ref[0, :, width + a : width + b],
                pad_s,
            ],
            axis=1,
        )

    def exchange(send, recv, sems, i):
        peer = (me_p + i) % (2 * LINE)
        return copy(send.at[peer], recv.at[me_p], sems.at[0, i], sems.at[1, i], {"patch": peer})

    def arrival(send, recv, sems, i):
        origin = (me_p - i + 2 * LINE) % (2 * LINE)
        return copy(send.at[origin], recv.at[origin], sems.at[0, i], sems.at[1, i], {"patch": origin})

    def start_exchange(send, recv, sems):
        recv[me_p] = send[me_p]

        def step(i, _):
            exchange(send, recv, sems, i).start()
            return 0

        lax.fori_loop(1, 2 * LINE, step, 0)

    def end_exchange(send, recv, sems):
        def step(i, _):
            arrival(send, recv, sems, i).wait_recv()
            return 0

        lax.fori_loop(1, 2 * LINE, step, 0)

    def drain_exchange(send, recv, sems):
        def step(i, _):
            exchange(send, recv, sems, i).wait_send()
            return 0

        lax.fori_loop(1, 2 * LINE, step, 0)

    to_twin.wait_recv()
    to_twin.wait_send()
    sums = part.at[c]

    def add_twin(i, _):
        sums[i] = sums[i] + sib_part[i]
        return 0

    lax.fori_loop(0, LINE, add_twin, 0)

    def go_up(d, k):
        a, m = CUTS[k]
        cut = pl.ds(a, m)
        return copy(sums.at[d, cut], from_low.at[d, cut], low_sems.at[0, d, k], low_sems.at[1, d, k], upper)

    def go_down(d, k):
        a, m = CUTS[k]
        cut = pl.ds(a, m)
        return copy(sums.at[d, cut], from_high.at[d, cut], high_sems.at[0, d, k], high_sems.at[1, d, k], lower)

    def reduce_step(t, _):
        for k, (a, m) in enumerate(CUTS):
            cut = pl.ds(a, m)

            @pl.when(t >= u)
            def _():
                d = LINE - 1 - t + u

                @pl.when(u > 0)
                def _():
                    go_up(d, k).wait_recv()
                    sums[d, cut] = sums[d, cut] + from_low[d, cut]

                @pl.when(d > u)
                def _():
                    go_up(d, k).start()

            @pl.when(t >= LINE - 1 - u)
            def _():
                d = t - (LINE - 1) + u

                @pl.when(u < LINE - 1)
                def _():
                    go_down(d, k).wait_recv()
                    sums[d, cut] = sums[d, cut] + from_high[d, cut]

                @pl.when(d < u)
                def _():
                    go_down(d, k).start()

        return 0

    lax.fori_loop(0, LINE, reduce_step, 0)

    piece = jax.nn.gelu(sums[u], approximate=True).astype(jnp.bfloat16)
    routed[x, h] = piece
    to_half = copy(routed.at[x, h], routed.at[x, h], h_sems.at[0], h_sems.at[1], half_peer)
    to_half.start()

    def x_copy(i, half):
        return copy(routed.at[x, half], routed.at[x, half], x_sems.at[0, half, i], x_sems.at[1, half, i], x_peer(i))

    def x_arrival(i, half):
        origin = (x - i + n_x) % n_x
        return copy(routed.at[x, half], routed.at[origin, half], x_sems.at[0, half, i], x_sems.at[1, half, i], x_peer(i))

    for i in range(1, n_x):
        x_copy(i, h).start()
    start_exchange(cq_send, cq_recv, cq_sems)
    start_exchange(sf_send, sf_recv, sf_sems)
    half_in = copy(routed.at[x, 1 - h], routed.at[x, 1 - h], h_sems.at[0], h_sems.at[1], half_peer)
    half_in.wait_recv()
    for i in range(1, n_x):
        x_copy(i, 1 - h).start()
    for i in range(1, n_x):
        x_arrival(i, h).wait_recv()
        x_arrival(i, 1 - h).wait_recv()

    def wanted(i):
        target = ((y + i) % n_y) * (n_h * n_x) + h * n_x + x
        source = route_ref[target]
        return routed[lax.rem(source, n_x), lax.rem(lax.div(source, n_x), n_h)]

    def y_copy(i):
        return copy(y_send.at[i], y_recv.at[y], y_sems.at[0, i], y_sems.at[1, i], y_peer(i))

    def y_arrival(i):
        return copy(y_send.at[i], y_recv.at[(y - i + n_y) % n_y], y_sems.at[0, i], y_sems.at[1, i], y_peer(i))

    for i in range(1, n_y):
        y_send[i] = wanted(i)
        y_copy(i).start()
    y_recv[y] = wanted(0)
    for i in range(1, n_y):
        y_arrival(i).wait_recv()
    source = route_ref[me_r]
    caption[c, u] = y_recv[lax.div(source, n_h * n_x)]

    def to_upper(q, k):
        a, m = CUTS[k]
        ref = caption.at[c, q, pl.ds(a, m)]
        return copy(ref, ref, up_sems.at[q, k], gather_recv.at[q, k], upper)

    def to_lower(q, k):
        a, m = CUTS[k]
        ref = caption.at[c, q, pl.ds(a, m)]
        return copy(ref, ref, down_sems.at[q, k], gather_recv.at[q, k], lower)

    def to_other_core(core, q, k):
        a, m = CUTS[k]
        ref = caption.at[core, q, pl.ds(a, m)]
        return copy(ref, ref, twin_sems.at[0, q, k], twin_sems.at[1, q, k], twin)

    def gather_step(t, _):
        for k in range(len(CUTS)):

            @pl.when(t <= u)
            def _():
                q = u - t

                @pl.when(t > 0)
                def _():
                    to_upper(q, k).wait_recv()

                @pl.when(u < LINE - 1)
                def _():
                    to_upper(q, k).start()

                to_other_core(c, q, k).start()

            @pl.when(t <= LINE - 1 - u)
            def _():
                q = u + t

                @pl.when(t > 0)
                def _():
                    to_lower(q, k).wait_recv()

                @pl.when(u > 0)
                def _():
                    to_lower(q, k).start()

                @pl.when(t > 0)
                def _():
                    to_other_core(c, q, k).start()

        return 0

    lax.fori_loop(0, LINE, gather_step, 0)

    end_exchange(sf_send, sf_recv, sf_sems)
    seq = 2 * LINE * tok
    whole = sf_recv[...].reshape(seq, 3 * LANES)
    queries, keys, values = whole[:, :HD], whole[:, HD : 2 * HD], whole[:, 2 * HD : 3 * HD]
    new_keys, new_values = whole[:, 3 * HD : 4 * HD], whole[:, 4 * HD : 5 * HD]
    contract_last = (((1,), (1,)), ((), ()))
    chunk = LANES
    own = (
        lax.broadcasted_iota(jnp.int32, (chunk, chunk), 0) // tok
        == lax.broadcasted_iota(jnp.int32, (chunk, chunk), 1) // tok
    )
    zero = jnp.zeros((), jnp.bfloat16)

    def blended(scores, head_values):
        weights = jnp.exp(scores - jnp.max(scores, axis=-1, keepdims=True))
        return weights, jnp.sum(weights, axis=-1, keepdims=True)

    out_pad = jnp.zeros((chunk, LANES - HD), jnp.bfloat16)
    per = chunk // tok
    for i in range(seq // chunk):
        a, b = i * chunk, (i + 1) * chunk
        scores = lax.dot_general(queries[a:b], keys, contract_last, preferred_element_type=jnp.float32)
        mine = lax.dot_general(queries[a:b], new_keys[a:b], contract_last, preferred_element_type=jnp.float32)
        mixed = [jnp.where(own, mine, scores[:, a:b])]
        if a > 0:
            mixed = [scores[:, :a]] + mixed
        if b < seq:
            mixed = mixed + [scores[:, b:]]
        scores = jnp.concatenate(mixed, axis=1) * HD ** (-0.5)
        weights, total = blended(scores, values)
        weights = weights.astype(jnp.bfloat16)
        near = weights[:, a:b]
        mixed = [jnp.where(own, zero, near)]
        if a > 0:
            mixed = [weights[:, :a]] + mixed
        if b < seq:
            mixed = mixed + [weights[:, b:]]
        result = jnp.dot(jnp.concatenate(mixed, axis=1), values, preferred_element_type=jnp.float32)
        result = result + jnp.dot(
            jnp.where(own, near, zero), new_values[a:b], preferred_element_type=jnp.float32
        )
        result = (result / total).astype(jnp.bfloat16)
        so_send[i * per : (i + 1) * per] = jnp.concatenate([result, out_pad], axis=1).reshape(per, tok, LANES)
    start_exchange(so_send, so_recv, so_sems)

    end_exchange(cq_send, cq_recv, cq_sems)

    def twin_wait(q, _):
        for k in range(len(CUTS)):
            to_other_core(1 - c, q, k).wait_recv()
        return 0

    lax.fori_loop(0, LINE, twin_wait, 0)
    caption_rows = jnp.concatenate(
        [jnp.concatenate([caption[place(i, j)] for j in range(col_tiles)], axis=1) for i in range(row_tiles)], axis=0
    )
    head_states = jnp.dot(caption_rows, kv_w_ref[...], preferred_element_type=jnp.float32).astype(jnp.bfloat16)
    prompt_keys, prompt_values = head_states[:, :HD], head_states[:, HD : 2 * HD]
    length = lengths_ref[source]
    visible = lax.broadcasted_iota(jnp.int32, (1, row_tiles * TILE), 1) < length
    cross_rows = cq_recv[...].reshape(seq, LANES)[:, :HD]
    for i in range(seq // chunk):
        a, b = i * chunk, (i + 1) * chunk
        scores = lax.dot_general(cross_rows[a:b], prompt_keys, contract_last, preferred_element_type=jnp.float32)
        scores = jnp.where(visible, scores * HD ** (-0.5), masked_score)
        weights, total = blended(scores, prompt_values)
        result = jnp.dot(weights.astype(jnp.bfloat16), prompt_values, preferred_element_type=jnp.float32)
        result = (result / total).astype(jnp.bfloat16)
        co_send[i * per : (i + 1) * per] = jnp.concatenate([result, out_pad], axis=1).reshape(per, tok, LANES)
    start_exchange(co_send, co_recv, co_sems)

    end_exchange(so_send, so_recv, so_sems)
    self_out_ref[0] = jnp.concatenate([so_recv[n][:, :HD].astype(jnp.float32) for n in range(HEADS)], axis=1)
    end_exchange(co_send, co_recv, co_sems)
    cross_out_ref[0] = jnp.concatenate([co_recv[n][:, :HD].astype(jnp.float32) for n in range(HEADS)], axis=1)

    for k in range(len(CUTS)):

        def drain(q, _):
            @pl.when(q > u)
            def _():
                go_up(q, k).wait_send()

            @pl.when(q < u)
            def _():
                go_down(q, k).wait_send()

            @pl.when((q <= u) & (u < LINE - 1))
            def _():
                to_upper(q, k).wait_send()

            @pl.when((q >= u) & (u > 0))
            def _():
                to_lower(q, k).wait_send()

            to_other_core(c, q, k).wait_send()
            return 0

        lax.fori_loop(0, LINE, drain, 0)
    to_half.wait_send()
    for i in range(1, n_x):
        x_copy(i, h).wait_send()
        x_copy(i, 1 - h).wait_send()
    for i in range(1, n_y):
        y_copy(i).wait_send()
    drain_exchange(cq_send, cq_recv, cq_sems)
    drain_exchange(sf_send, sf_recv, sf_sems)
    drain_exchange(so_send, so_recv, so_sems)
    drain_exchange(co_send, co_recv, co_sems)


def shards(
    dims,
    image_queries,
    cross_queries,
    fresh_kv,
    stale_kv,
    prompt_states,
    caption_weight,
    cross_kv_weight,
    prompt_lengths,
    prompt_route,
):
    n_y, n_h, n_x = dims
    tok, width = image_queries.shape[1:]
    piece = (TILES, TILE, LANES)
    dma = pltpu.SemaphoreType.DMA
    vmem = pl.BlockSpec(memory_space=pltpu.VMEM)
    smem = pl.BlockSpec(memory_space=pltpu.SMEM)
    f32, bf16 = jnp.float32, jnp.bfloat16
    lines = (LINE, len(CUTS))
    by_head = pltpu.VMEM((HEADS, tok, LANES), bf16)
    by_head_wide = pltpu.VMEM((HEADS, tok, 3 * LANES), bf16)
    return pl.pallas_call(
        functools.partial(kernel, dims),
        out_shape=[jax.ShapeDtypeStruct((1, tok, width), f32)] * 2,
        in_specs=[smem, smem] + [vmem] * 7,
        out_specs=[vmem, vmem],
        scratch_shapes=[
            pltpu.VMEM((2, LINE, *piece), f32),
            pltpu.VMEM((LINE, *piece), f32),
            pltpu.VMEM((LINE, *piece), f32),
            pltpu.VMEM((LINE, *piece), f32),
            pltpu.VMEM((n_x, n_h, *piece), bf16),
            pltpu.VMEM((n_y, *piece), bf16),
            pltpu.VMEM((n_y, *piece), bf16),
            pltpu.VMEM((2, LINE, *piece), bf16),
            by_head,
            by_head,
            by_head_wide,
            by_head_wide,
            by_head,
            by_head,
            by_head,
            by_head,
            dma((2,)),
            dma((2, *lines)),
            dma((2, *lines)),
            dma((2,)),
            dma((2, n_h, n_x)),
            dma((2, n_y)),
            dma(lines),
            dma(lines),
            dma(lines),
            dma((2, *lines)),
            dma((2, HEADS)),
            dma((2, HEADS)),
            dma((2, HEADS)),
            dma((2, HEADS)),
        ],
        compiler_params=pltpu.CompilerParams(
            collective_id=0, has_side_effects=True, vmem_limit_bytes=48 * 1024 * 1024
        ),
    )(
        prompt_route,
        prompt_lengths,
        prompt_states,
        caption_weight,
        cross_kv_weight,
        image_queries,
        cross_queries,
        fresh_kv,
        stale_kv,
    )


def solution(mesh, dims=(4, 2, 4)):
    in_specs = (
        P("req", "patch", None),
        P("req", "patch", None),
        P("req", "patch", None),
        P("req", "patch", None),
        P("req", None, "patch"),
        P("patch", None),
        P(None, "patch"),
        P(),
        P(),
    )
    out_specs = (P("req", "patch", None), P("req", "patch", None))
    return jax.shard_map(
        functools.partial(shards, dims), mesh=mesh, in_specs=in_specs, out_specs=out_specs, check_vma=False
    )
```

time: 615 us -> 110 us (0.18)
  waiting for transfers between devices: 580 us -> 0 us
  Pallas kernels: 0 us -> 103 us
  between operations: 15.9 us -> 0.73 us
  matrix products: 8.64 us -> 0 us
    all_gather x3 -> x0, waiting for transfers between devices: 383 us -> none  [the longest x1 188 us: shards(): all_prompts = lax.all_gather(prompt_states, 'req', axis=0, tiled=True)]
    psum x1 -> x0, waiting for transfers between devices: 196 us -> none  [shards(): summed = lax.psum(partial_sum, 'patch')]
    pallas_call x0 -> x1, Pallas kernels: none -> 103 us  [shards(): pl.pallas_call(functools.partial(kernel, dims), out_shape=[jax.ShapeDtype...]
    dot_general x8 -> x0, matrix products: 8.64 us -> none  [the longest x1 2.65 us: shards(): jnp.dot(caption, cross_kv_weight, preferred_element_type=jnp.float32)]
  transfers between devices with their start and end apart: 4 -> 0, of which waited for: 4 -> 0; matrix products, arithmetic and copies ran while one was open for 2% -> 0% of each run, Pallas kernels for 0% -> 0%
where the time goes in v1:
time: 110 us; the launch traced here: 109 us
  Pallas kernels  103 us (94%)
  local copies, waits for them, and re-layouts  5.31 us (5%)
    pallas_call x1, Pallas kernels, shards(): pl.pallas_call(functools.partial(kernel, dims), out_shape=[jax.ShapeDtype...  103 us
    unnamed x19, local copies, waits for them, and re-layouts  5.31 us

profile of v1, /device:TPU:1, one launch (start us, length us, event | category | flops | bytes accessed | tf_op | source)
XLA Modules:
  0.0 109.4 jit_solution(15219484007013263861)
XLA Ops:
  0.6 0.0 copy-start.6
  0.6 0.0 copy-start.7
  0.7 0.0 copy-start
  0.7 0.0 copy-start.1
  0.7 0.0 copy-start.2
  0.7 1.3 %copy.11.kv_w_ref = bf16[1152,144]{1,0:T(8,128)(2,1)S(1)} copy(bf16[1152,144]{0,1:T(8,128)(2,1)} %param.15) | data formatting | bytes 663552 | tf_op args[6]
  2.0 0.0 copy-done.6
  2.0 0.0 copy-done.7
  2.0 0.0 copy-done
  2.0 0.0 copy-done.1
  2.0 0.0 copy-done.2
  2.0 0.0 copy-start.3
  2.0 0.9 copy-done.3
  2.9 0.0 copy-start.4
  2.9 0.9 copy-done.4
  3.8 0.0 copy-start.5
  3.8 0.9 copy-done.5
  4.7 103.4 %shard_map.104 = (f32[1,32,1152]{2,1,0:T(8,128)S(1)}, f32[1,32,1152]{2,1,0:T(8,128)S(1)}) custom-call(s32[32]{0:T(128)S(1)} %copy-done.6, s32[32]{0:T(128)S(1)} %copy-done.7, bf16[1,300,256]{2,1,0:T(8,128)(2,1)S(1)} %copy-done.1, bf16[256,1152]{1,0:T(8,128)(2,1)S(1)} %copy-done, bf16[1152,144]{1,0:T(8,128)(2,1)S(1)} %copy.11.kv_w_ref, ...), custom_call_target="tpu_custom_call" | custom-call | tf_op jit(solution)/shard_map/pallas_call | solution.py:468
  108.1 0.7 copy.14
  108.8 0.7 copy.15
Async XLA Ops:
  0.6 1.3 %copy-start.6 = (s32[32]{0:T(128)S(1)}, s32[32]{0:T(128)}, u32[]{:S(2)}) copy-start(s32[32]{0:T(128)} %route_ref.1) | copy-start | bytes 388
  0.6 1.3 %copy-start.7 = (s32[32]{0:T(128)S(1)}, s32[32]{0:T(128)}, u32[]{:S(2)}) copy-start(s32[32]{0:T(128)} %lengths_ref.1) | copy-start | bytes 388
  0.7 1.3 %copy-start = (bf16[256,1152]{1,0:T(8,128)(2,1)S(1)}, bf16[256,1152]{1,0:T(8,128)(2,1)}, u32[]{:S(2)}) copy-start(bf16[256,1152]{1,0:T(8,128)(2,1)} %caption_w_ref.1) | copy-start | bytes 1769476
  0.7 1.3 %copy-start.1 = (bf16[1,300,256]{2,1,0:T(8,128)(2,1)S(1)}, bf16[1,300,256]{2,1,0:T(8,128)(2,1)}, u32[]{:S(2)}) copy-start(bf16[1,300,256]{2,1,0:T(8,128)(2,1)} %prompt_ref.1) | copy-start | bytes 460804
  0.7 1.3 %copy-start.2 = (bf16[1,32,2304]{2,1,0:T(8,128)(2,1)S(1)}, bf16[1,32,2304]{2,1,0:T(8,128)(2,1)}, u32[]{:S(2)}) copy-start(bf16[1,32,2304]{2,1,0:T(8,128)(2,1)} %fresh_ref.1) | copy-start | bytes 442372
  2.0 0.9 copy-start.3
  2.9 0.9 copy-start.4
  3.8 0.9 copy-start.5

commit v2 on v1

--- a/solution.py
+++ b/solution.py
@@ -13,6 +13,8 @@
 TILE = 16
 TILES = 11
 LINE = 8
+HALF = LINE // 2
+SUM_CUTS = ((0, 3), (3, 3), (6, 3), (9, 2))
 CUTS = ((0, 6), (6, 5))
 masked_score = -1e30
 MESH = pl.DeviceIdType.MESH
@@ -22,6 +24,15 @@
     dims,
     route_ref,
     lengths_ref,
+    prompt_hbm,
+    caption_w_hbm,
+    kv_w_hbm,
+    image_q_hbm,
+    cross_q_hbm,
+    fresh_hbm,
+    stale_hbm,
+    self_out_ref,
+    cross_out_ref,
     prompt_ref,
     caption_w_ref,
     kv_w_ref,
@@ -29,8 +40,6 @@
     cross_q_ref,
     fresh_ref,
     stale_ref,
-    self_out_ref,
-    cross_out_ref,
     part,
     sib_part,
     from_low,
@@ -47,14 +56,14 @@
     so_recv,
     co_send,
     co_recv,
+    load_sems,
     sib_sems,
     low_sems,
     high_sems,
     h_sems,
     x_sems,
     y_sems,
-    up_sems,
-    down_sems,
+    gather_send,
     gather_recv,
     twin_sems,
     cq_sems,
@@ -70,18 +79,19 @@
     x = me_r % n_x
     z = me_p // 2
     c = me_p % 2
-    u = z + h * (LINE - 1 - 2 * z)
-
-    def on_line(pos, core):
-        return 2 * (pos + h * (LINE - 1 - 2 * pos)) + core
+    u = z
+    shift = h * HALF
+
+    def piece_of(pos):
+        return (pos + shift) % LINE
 
     def patch_peer(i):
         return {"patch": (me_p + i) % (2 * LINE)}
 
     twin = {"patch": 2 * z + 1 - c}
-    upper = {"patch": on_line(jnp.minimum(u + 1, LINE - 1), c)}
-    lower = {"patch": on_line(jnp.maximum(u - 1, 0), c)}
-    half_peer = {"req": me_r + n_x * (1 - 2 * h), "patch": 2 * (LINE - 1 - z) + c}
+    upper = {"patch": 2 * jnp.minimum(u + 1, LINE - 1) + c}
+    lower = {"patch": 2 * jnp.maximum(u - 1, 0) + c}
+    half_peer = {"req": me_r + n_x * (1 - 2 * h), "patch": 2 * ((z + HALF) % LINE) + c}
 
     def x_peer(i):
         return {"req": me_r - x + (x + i) % n_x}
@@ -94,6 +104,20 @@
             src_ref=src, dst_ref=dst, send_sem=send, recv_sem=recv, device_id=device, device_id_type=MESH
         )
 
+    loads = [
+        pltpu.make_async_copy(src, dst, load_sems.at[i])
+        for i, (src, dst) in enumerate(
+            (
+                (prompt_hbm, prompt_ref),
+                (caption_w_hbm, caption_w_ref),
+                (cross_q_hbm, cross_q_ref),
+                (image_q_hbm, image_q_ref),
+                (stale_hbm, stale_ref),
+                (fresh_hbm, fresh_ref),
+                (kv_w_hbm, kv_w_ref),
+            )
+        )
+    ]
     barrier = pltpu.get_barrier_semaphore()
     greeted = 0
     for device in (
@@ -104,8 +128,11 @@
     ):
         pl.semaphore_signal(barrier, inc=1, device_id=device, device_id_type=MESH)
         greeted += 1
-    pl.semaphore_wait(barrier, greeted)
-
+    for load in loads:
+        load.start()
+
+    loads[0].wait()
+    loads[1].wait()
     prompt = prompt_ref[0]
     rows = prompt.shape[0]
     row_tiles = -(-rows // TILE)
@@ -119,6 +146,8 @@
         piece, at = divmod(i * col_tiles + j, TILES)
         return piece // LINE, piece % LINE, at
 
+    slots = [piece_of(g) for g in range(LINE)]
+
     group = 3
     for j0 in range(0, col_tiles, group):
         block = jnp.dot(
@@ -126,12 +155,16 @@
         )
         for i in range(row_tiles):
             for j in range(group):
-                part[place(i, j0 + j)] = block[i * TILE : (i + 1) * TILE, j * LANES : (j + 1) * LANES]
+                core, g, at = place(i, j0 + j)
+                part[core, slots[g], at] = block[i * TILE : (i + 1) * TILE, j * LANES : (j + 1) * LANES]
     for t in range(row_tiles * col_tiles, 2 * LINE * TILES):
-        part[t // (LINE * TILES), (t // TILES) % LINE, t % TILES] = jnp.zeros((TILE, LANES), jnp.float32)
+        part[t // (LINE * TILES), slots[(t // TILES) % LINE], t % TILES] = jnp.zeros((TILE, LANES), jnp.float32)
 
     to_twin = copy(part.at[1 - c], sib_part, sib_sems.at[0], sib_sems.at[1], twin)
+    pl.semaphore_wait(barrier, greeted)
     to_twin.start()
+    for load in loads[2:]:
+        load.wait()
 
     tok = image_q_ref.shape[1]
     pad_c = jnp.zeros((tok, LANES - HD), jnp.bfloat16)
@@ -182,6 +215,8 @@
 
         lax.fori_loop(1, 2 * LINE, step, 0)
 
+    start_exchange(cq_send, cq_recv, cq_sems)
+    start_exchange(sf_send, sf_recv, sf_sems)
     to_twin.wait_recv()
     to_twin.wait_send()
     sums = part.at[c]
@@ -193,17 +228,17 @@
     lax.fori_loop(0, LINE, add_twin, 0)
 
     def go_up(d, k):
-        a, m = CUTS[k]
+        a, m = SUM_CUTS[k]
         cut = pl.ds(a, m)
         return copy(sums.at[d, cut], from_low.at[d, cut], low_sems.at[0, d, k], low_sems.at[1, d, k], upper)
 
     def go_down(d, k):
-        a, m = CUTS[k]
+        a, m = SUM_CUTS[k]
         cut = pl.ds(a, m)
         return copy(sums.at[d, cut], from_high.at[d, cut], high_sems.at[0, d, k], high_sems.at[1, d, k], lower)
 
     def reduce_step(t, _):
-        for k, (a, m) in enumerate(CUTS):
+        for k, (a, m) in enumerate(SUM_CUTS):
             cut = pl.ds(a, m)
 
             @pl.when(t >= u)
@@ -236,101 +271,83 @@
 
     lax.fori_loop(0, LINE, reduce_step, 0)
 
-    piece = jax.nn.gelu(sums[u], approximate=True).astype(jnp.bfloat16)
-    routed[x, h] = piece
-    to_half = copy(routed.at[x, h], routed.at[x, h], h_sems.at[0], h_sems.at[1], half_peer)
-    to_half.start()
-
-    def x_copy(i, half):
-        return copy(routed.at[x, half], routed.at[x, half], x_sems.at[0, half, i], x_sems.at[1, half, i], x_peer(i))
-
-    def x_arrival(i, half):
-        origin = (x - i + n_x) % n_x
-        return copy(routed.at[x, half], routed.at[origin, half], x_sems.at[0, half, i], x_sems.at[1, half, i], x_peer(i))
-
-    for i in range(1, n_x):
-        x_copy(i, h).start()
-    start_exchange(cq_send, cq_recv, cq_sems)
-    start_exchange(sf_send, sf_recv, sf_sems)
-    half_in = copy(routed.at[x, 1 - h], routed.at[x, 1 - h], h_sems.at[0], h_sems.at[1], half_peer)
-    half_in.wait_recv()
-    for i in range(1, n_x):
-        x_copy(i, 1 - h).start()
-    for i in range(1, n_x):
-        x_arrival(i, h).wait_recv()
-        x_arrival(i, 1 - h).wait_recv()
-
-    def wanted(i):
-        target = ((y + i) % n_y) * (n_h * n_x) + h * n_x + x
-        source = route_ref[target]
-        return routed[lax.rem(source, n_x), lax.rem(lax.div(source, n_x), n_h)]
-
-    def y_copy(i):
-        return copy(y_send.at[i], y_recv.at[y], y_sems.at[0, i], y_sems.at[1, i], y_peer(i))
-
-    def y_arrival(i):
-        return copy(y_send.at[i], y_recv.at[(y - i + n_y) % n_y], y_sems.at[0, i], y_sems.at[1, i], y_peer(i))
-
-    for i in range(1, n_y):
-        y_send[i] = wanted(i)
-        y_copy(i).start()
-    y_recv[y] = wanted(0)
-    for i in range(1, n_y):
-        y_arrival(i).wait_recv()
+    def to_half(k):
+        ref = routed[k].at[x, h]
+        return copy(ref, ref, h_sems.at[0, k], h_sems.at[1, k], half_peer)
+
+    def half_arrival(k):
+        ref = routed[k].at[x, 1 - h]
+        return copy(ref, ref, h_sems.at[0, k], h_sems.at[1, k], half_peer)
+
+    def x_copy(i, half, k):
+        ref = routed[k].at[x, half]
+        return copy(ref, ref, x_sems.at[0, k, half, i], x_sems.at[1, k, half, i], x_peer(i))
+
+    def x_arrival(i, half, k):
+        ref = routed[k].at[(x - i + n_x) % n_x, half]
+        return copy(ref, ref, x_sems.at[0, k, half, i], x_sems.at[1, k, half, i], x_peer(i))
+
+    def wanted(i, k):
+        source = route_ref[((y + i) % n_y) * (n_h * n_x) + h * n_x + x]
+        return routed[k][lax.rem(source, n_x), lax.rem(lax.div(source, n_x), n_h)]
+
+    def y_copy(i, k):
+        return copy(y_send[k].at[i], y_recv[k].at[y], y_sems.at[0, k, i], y_sems.at[1, k, i], y_peer(i))
+
+    def y_arrival(i, k):
+        ref = y_recv[k].at[(y - i + n_y) % n_y]
+        return copy(ref, ref, y_sems.at[0, k, i], y_sems.at[1, k, i], y_peer(i))
+
+    here = piece_of(u)
+    there = piece_of((u + HALF) % LINE)
+
+    def beside(i):
+        return (u // HALF) * HALF + (u + i) % HALF
+
+    def tiles_of(core, g, k):
+        a, m = CUTS[k]
+        return caption.at[core, g, pl.ds(a, m)]
+
+    def spread(g, i, n, k):
+        pos = beside(i) if i else (u + HALF) % LINE
+        ref = tiles_of(c, g, k)
+        return copy(ref, ref, gather_send.at[n, k], gather_recv.at[g, k], {"patch": 2 * pos + c})
+
+    def gathered(g, k):
+        ref = tiles_of(c, g, k)
+        return copy(ref, ref, gather_send.at[0, k], gather_recv.at[g, k], twin)
+
+    def to_other_core(core, g, k):
+        ref = tiles_of(core, g, k)
+        return copy(ref, ref, twin_sems.at[0, g, k], twin_sems.at[1, g, k], twin)
+
+    cuts = range(len(CUTS))
+    for k, (a, m) in enumerate(CUTS):
+        piece = jax.nn.gelu(sums[u, a : a + m], approximate=True).astype(jnp.bfloat16)
+        routed[k][x, h] = piece
+        to_half(k).start()
+        for i in range(1, n_x):
+            x_copy(i, h, k).start()
+    for k in cuts:
+        half_arrival(k).wait_recv()
+        for i in range(1, n_x):
+            x_copy(i, 1 - h, k).start()
+    for k in cuts:
+        for i in range(1, n_x):
+            x_arrival(i, h, k).wait_recv()
+            x_arrival(i, 1 - h, k).wait_recv()
+        for i in range(1, n_y):
+            y_send[k][i] = wanted(i, k)
+            y_copy(i, k).start()
+        y_recv[k][y] = wanted(0, k)
     source = route_ref[me_r]
-    caption[c, u] = y_recv[lax.div(source, n_h * n_x)]
-
-    def to_upper(q, k):
-        a, m = CUTS[k]
-        ref = caption.at[c, q, pl.ds(a, m)]
-        return copy(ref, ref, up_sems.at[q, k], gather_recv.at[q, k], upper)
-
-    def to_lower(q, k):
-        a, m = CUTS[k]
-        ref = caption.at[c, q, pl.ds(a, m)]
-        return copy(ref, ref, down_sems.at[q, k], gather_recv.at[q, k], lower)
-
-    def to_other_core(core, q, k):
-        a, m = CUTS[k]
-        ref = caption.at[core, q, pl.ds(a, m)]
-        return copy(ref, ref, twin_sems.at[0, q, k], twin_sems.at[1, q, k], twin)
-
-    def gather_step(t, _):
-        for k in range(len(CUTS)):
-
-            @pl.when(t <= u)
-            def _():
-                q = u - t
-
-                @pl.when(t > 0)
-                def _():
-                    to_upper(q, k).wait_recv()
-
-                @pl.when(u < LINE - 1)
-                def _():
-                    to_upper(q, k).start()
-
-                to_other_core(c, q, k).start()
-
-            @pl.when(t <= LINE - 1 - u)
-            def _():
-                q = u + t
-
-                @pl.when(t > 0)
-                def _():
-                    to_lower(q, k).wait_recv()
-
-                @pl.when(u > 0)
-                def _():
-                    to_lower(q, k).start()
-
-                @pl.when(t > 0)
-                def _():
-                    to_other_core(c, q, k).start()
-
-        return 0
-
-    lax.fori_loop(0, LINE, gather_step, 0)
+    for k, (a, m) in enumerate(CUTS):
+        for i in range(1, n_y):
+            y_arrival(i, k).wait_recv()
+        caption[c, here, a : a + m] = y_recv[k][lax.div(source, n_h * n_x)]
+        for i in range(HALF):
+            spread(here, i, i, k).start()
+        to_other_core(c, here, k).start()
 
     end_exchange(sf_send, sf_recv, sf_sems)
     seq = 2 * LINE * tok
@@ -377,6 +394,18 @@
         so_send[i * per : (i + 1) * per] = jnp.concatenate([result, out_pad], axis=1).reshape(per, tok, LANES)
     start_exchange(so_send, so_recv, so_sems)
 
+    for k in cuts:
+        gathered(there, k).wait_recv()
+        for i in range(1, HALF):
+            spread(there, i, HALF - 1 + i, k).start()
+        to_other_core(c, there, k).start()
+    for far in (0, HALF):
+        for k in cuts:
+            for i in range(1, HALF):
+                g = piece_of((beside(i) + far) % LINE)
+                gathered(g, k).wait_recv()
+                to_other_core(c, g, k).start()
+
     end_exchange(cq_send, cq_recv, cq_sems)
 
     def twin_wait(q, _):
@@ -388,7 +417,9 @@
     caption_rows = jnp.concatenate(
         [jnp.concatenate([caption[place(i, j)] for j in range(col_tiles)], axis=1) for i in range(row_tiles)], axis=0
     )
-    head_states = jnp.dot(caption_rows, kv_w_ref[...], preferred_element_type=jnp.float32).astype(jnp.bfloat16)
+    head_states = lax.dot_general(
+        caption_rows, kv_w_ref[...], contract_last, preferred_element_type=jnp.float32
+    ).astype(jnp.bfloat16)
     prompt_keys, prompt_values = head_states[:, :HD], head_states[:, HD : 2 * HD]
     length = lengths_ref[source]
     visible = lax.broadcasted_iota(jnp.int32, (1, row_tiles * TILE), 1) < length
@@ -408,7 +439,7 @@
     end_exchange(co_send, co_recv, co_sems)
     cross_out_ref[0] = jnp.concatenate([co_recv[n][:, :HD].astype(jnp.float32) for n in range(HEADS)], axis=1)
 
-    for k in range(len(CUTS)):
+    for k in range(len(SUM_CUTS)):
 
         def drain(q, _):
             @pl.when(q > u)
@@ -419,24 +450,26 @@
             def _():
                 go_down(q, k).wait_send()
 
-            @pl.when((q <= u) & (u < LINE - 1))
-            def _():
-                to_upper(q, k).wait_send()
-
-            @pl.when((q >= u) & (u > 0))
-            def _():
-                to_lower(q, k).wait_send()
-
-            to_other_core(c, q, k).wait_send()
             return 0
 
         lax.fori_loop(0, LINE, drain, 0)
-    to_half.wait_send()
-    for i in range(1, n_x):
-        x_copy(i, h).wait_send()
-        x_copy(i, 1 - h).wait_send()
-    for i in range(1, n_y):
-        y_copy(i).wait_send()
+    for k in cuts:
+        to_half(k).wait_send()
+        for i in range(1, n_x):
+            x_copy(i, h, k).wait_send()
+            x_copy(i, 1 - h, k).wait_send()
+        for i in range(1, n_y):
+            y_copy(i, k).wait_send()
+        for i in range(HALF):
+            spread(here, i, i, k).wait_send()
+        for i in range(1, HALF):
+            spread(there, i, HALF - 1 + i, k).wait_send()
+
+        def drain_twin(g, _):
+            to_other_core(c, g, k).wait_send()
+            return 0
+
+        lax.fori_loop(0, LINE, drain_twin, 0)
     drain_exchange(cq_send, cq_recv, cq_sems)
     drain_exchange(sf_send, sf_recv, sf_sems)
     drain_exchange(so_send, so_recv, so_sems)
@@ -456,28 +489,39 @@
     prompt_route,
 ):
     n_y, n_h, n_x = dims
+    operands = (
+        prompt_states,
+        caption_weight,
+        cross_kv_weight.T,
+        image_queries,
+        cross_queries,
+        fresh_kv,
+        stale_kv,
+    )
     tok, width = image_queries.shape[1:]
     piece = (TILES, TILE, LANES)
     dma = pltpu.SemaphoreType.DMA
     vmem = pl.BlockSpec(memory_space=pltpu.VMEM)
     smem = pl.BlockSpec(memory_space=pltpu.SMEM)
     f32, bf16 = jnp.float32, jnp.bfloat16
-    lines = (LINE, len(CUTS))
+    sum_lines, lines, cuts = (LINE, len(SUM_CUTS)), (LINE, len(CUTS)), len(CUTS)
+    hbm = pl.BlockSpec(memory_space=pltpu.HBM)
     by_head = pltpu.VMEM((HEADS, tok, LANES), bf16)
     by_head_wide = pltpu.VMEM((HEADS, tok, 3 * LANES), bf16)
     return pl.pallas_call(
         functools.partial(kernel, dims),
         out_shape=[jax.ShapeDtypeStruct((1, tok, width), f32)] * 2,
-        in_specs=[smem, smem] + [vmem] * 7,
+        in_specs=[smem, smem] + [hbm] * 7,
         out_specs=[vmem, vmem],
         scratch_shapes=[
+            *(pltpu.VMEM(array.shape, bf16) for array in operands),
             pltpu.VMEM((2, LINE, *piece), f32),
             pltpu.VMEM((LINE, *piece), f32),
             pltpu.VMEM((LINE, *piece), f32),
             pltpu.VMEM((LINE, *piece), f32),
-            pltpu.VMEM((n_x, n_h, *piece), bf16),
-            pltpu.VMEM((n_y, *piece), bf16),
-            pltpu.VMEM((n_y, *piece), bf16),
+            [pltpu.VMEM((n_x, n_h, m, TILE, LANES), bf16) for _, m in CUTS],
+            [pltpu.VMEM((n_y, m, TILE, LANES), bf16) for _, m in CUTS],
+            [pltpu.VMEM((n_y, m, TILE, LANES), bf16) for _, m in CUTS],
             pltpu.VMEM((2, LINE, *piece), bf16),
             by_head,
             by_head,
@@ -487,14 +531,14 @@
             by_head,
             by_head,
             by_head,
+            dma((len(operands),)),
             dma((2,)),
-            dma((2, *lines)),
-            dma((2, *lines)),
-            dma((2,)),
-            dma((2, n_h, n_x)),
-            dma((2, n_y)),
-            dma(lines),
-            dma(lines),
+            dma((2, *sum_lines)),
+            dma((2, *sum_lines)),
+            dma((2, cuts)),
+            dma((2, cuts, n_h, n_x)),
+            dma((2, cuts, n_y)),
+            dma((LINE - 1, cuts)),
             dma(lines),
             dma((2, *lines)),
             dma((2, HEADS)),
@@ -503,19 +547,9 @@
             dma((2, HEADS)),
         ],
         compiler_params=pltpu.CompilerParams(
-            collective_id=0, has_side_effects=True, vmem_limit_bytes=48 * 1024 * 1024
+            collective_id=0, has_side_effects=True, vmem_limit_bytes=60 * 1024 * 1024
         ),
-    )(
-        prompt_route,
-        prompt_lengths,
-        prompt_states,
-        caption_weight,
-        cross_kv_weight,
-        image_queries,
-        cross_queries,
-        fresh_kv,
-        stale_kv,
-    )
+    )(prompt_route, prompt_lengths, *operands)
 
 
 def solution(mesh, dims=(4, 2, 4)):

time: 110 us -> 97.9 us (0.89)
  Pallas kernels: 103 us -> 94.8 us
  local copies, waits for them, and re-layouts: 5.31 us -> 2.28 us
    pallas_call x1, Pallas kernels: 103 us -> 94.8 us  [shards(): pl.pallas_call(functools.partial(kernel, dims), out_shape=[jax.ShapeDtype...]
    unnamed x19 -> x4, local copies, waits for them, and re-layouts: 5.31 us -> 2.28 us
where the time goes in v2:
time: 97.9 us; the launch traced here: 97.8 us
  Pallas kernels  94.8 us (97%)
  local copies, waits for them, and re-layouts  2.28 us (2%)
    pallas_call x1, Pallas kernels, shards(): pl.pallas_call(functools.partial(kernel, dims), out_shape=[jax.ShapeDtype...  94.8 us
    unnamed x4, local copies, waits for them, and re-layouts  2.28 us

profile of v2, /device:TPU:1, one launch (start us, length us, event | category | flops | bytes accessed | tf_op | source)
XLA Modules:
  0.0 97.8 jit_solution(5590052058028448473)
XLA Ops:
  0.6 94.8 %shard_map.104 = (f32[1,32,1152]{2,1,0:T(8,128)}, f32[1,32,1152]{2,1,0:T(8,128)}) custom-call(s32[32]{0:T(128)} %route_ref.1, s32[32]{0:T(128)} %lengths_ref.1, bf16[1,300,256]{2,1,0:T(8,128)(2,1)} %prompt_hbm.1, bf16[256,1152]{1,0:T(8,128)(2,1)} %caption_w_hbm.1, bf16[144,1152]{1,0:T(8,128)(2,1)} %bitcast.1, bf16[1,32,1152]{2,1,0:T(8,128)(2,1)} %image_q_hbm.1, ...), custom_call_target="tpu_custom_call" | custom-call | tf_op jit(solution)/shard_map/pallas_call | solution.py:511
  95.5 0.0 copy-start
  95.5 1.6 %copy.13 = f32[1,32,1152]{2,1,0:T(8,128)} copy(f32[1,32,1152]{2,1,0:T(8,128)} %get-tuple-element.4) | data formatting | bytes 294912
  97.1 0.0 copy-done
  97.1 0.7 copy.14
Async XLA Ops:
  95.5 1.6 %copy-start = (f32[1,32,1152]{2,1,0:T(8,128)S(1)}, f32[1,32,1152]{2,1,0:T(8,128)}, u32[]{:S(2)}) copy-start(f32[1,32,1152]{2,1,0:T(8,128)} %get-tuple-element.5) | copy-start | bytes 442372

commit v3 on v2

--- a/solution.py
+++ b/solution.py
@@ -42,8 +42,9 @@
     stale_ref,
     part,
     sib_part,
-    from_low,
-    from_high,
+    running,
+    crossed,
+    terms,
     routed,
     y_send,
     y_recv,
@@ -56,10 +57,13 @@
     so_recv,
     co_send,
     co_recv,
+    fresh_stats,
+    fresh_blend,
     load_sems,
     sib_sems,
-    low_sems,
-    high_sems,
+    run_sems,
+    cross_sems,
+    term_sems,
     h_sems,
     x_sems,
     y_sems,
@@ -89,8 +93,6 @@
         return {"patch": (me_p + i) % (2 * LINE)}
 
     twin = {"patch": 2 * z + 1 - c}
-    upper = {"patch": 2 * jnp.minimum(u + 1, LINE - 1) + c}
-    lower = {"patch": 2 * jnp.maximum(u - 1, 0) + c}
     half_peer = {"req": me_r + n_x * (1 - 2 * h), "patch": 2 * ((z + HALF) % LINE) + c}
 
     def x_peer(i):
@@ -168,7 +170,7 @@
 
     tok = image_q_ref.shape[1]
     pad_c = jnp.zeros((tok, LANES - HD), jnp.bfloat16)
-    pad_s = jnp.zeros((tok, 3 * LANES - 5 * HD), jnp.bfloat16)
+    pad_s = jnp.zeros((tok, 2 * LANES - 3 * HD), jnp.bfloat16)
     for n in range(HEADS):
         a, b = n * HD, (n + 1) * HD
         cq_send[n] = jnp.concatenate([cross_q_ref[0, :, a:b], pad_c], axis=1)
@@ -177,8 +179,6 @@
                 image_q_ref[0, :, a:b],
                 stale_ref[0, :, a:b],
                 stale_ref[0, :, width + a : width + b],
-                fresh_ref[0, :, a:b],
-                fresh_ref[0, :, width + a : width + b],
                 pad_s,
             ],
             axis=1,
@@ -216,7 +216,6 @@
         lax.fori_loop(1, 2 * LINE, step, 0)
 
     start_exchange(cq_send, cq_recv, cq_sems)
-    start_exchange(sf_send, sf_recv, sf_sems)
     to_twin.wait_recv()
     to_twin.wait_send()
     sums = part.at[c]
@@ -227,49 +226,84 @@
 
     lax.fori_loop(0, LINE, add_twin, 0)
 
-    def go_up(d, k):
+    inner = HALF - 1
+    left = u < HALF
+    deep = jnp.where(left, u, LINE - 1 - u)
+
+    def at(pos):
+        return jnp.where(left, pos, LINE - 1 - pos)
+
+    def at_device(pos):
+        return {"patch": 2 * at(pos) + c}
+
+    def sum_cut(k):
         a, m = SUM_CUTS[k]
-        cut = pl.ds(a, m)
-        return copy(sums.at[d, cut], from_low.at[d, cut], low_sems.at[0, d, k], low_sems.at[1, d, k], upper)
-
-    def go_down(d, k):
-        a, m = SUM_CUTS[k]
-        cut = pl.ds(a, m)
-        return copy(sums.at[d, cut], from_high.at[d, cut], high_sems.at[0, d, k], high_sems.at[1, d, k], lower)
+        return pl.ds(a, m)
+
+    def inward(pos, k):
+        return copy(
+            sums.at[at(pos), sum_cut(k)],
+            running.at[at(pos), sum_cut(k)],
+            run_sems.at[0, pos, k],
+            run_sems.at[1, pos, k],
+            at_device(jnp.minimum(deep + 1, inner)),
+        )
+
+    def across(pos, k):
+        return copy(
+            sums.at[at(pos), sum_cut(k)],
+            crossed.at[sum_cut(k)],
+            cross_sems.at[0, pos, k],
+            cross_sems.at[1, 0, k],
+            at_device(pos),
+        )
+
+    def outward(pos):
+        return copy(
+            sums.at[at(pos)], terms.at[deep], term_sems.at[0, pos], term_sems.at[1, deep], at_device(pos)
+        )
+
+    def term_arrival(pos):
+        return copy(sums.at[u], terms.at[pos], term_sems.at[0, 0], term_sems.at[1, pos], at_device(pos))
+
+    for pos in range(inner):
+
+        @pl.when(pos < deep)
+        def _():
+            outward(pos).start()
 
     def reduce_step(t, _):
-        for k, (a, m) in enumerate(SUM_CUTS):
-            cut = pl.ds(a, m)
-
-            @pl.when(t >= u)
-            def _():
-                d = LINE - 1 - t + u
-
-                @pl.when(u > 0)
+        pos = LINE - 1 - t
+
+        @pl.when(pos >= deep)
+        def _():
+            for k in range(len(SUM_CUTS)):
+
+                @pl.when(deep > 0)
                 def _():
-                    go_up(d, k).wait_recv()
-                    sums[d, cut] = sums[d, cut] + from_low[d, cut]
-
-                @pl.when(d > u)
+                    inward(pos, k).wait_recv()
+                    sums[at(pos), sum_cut(k)] = sums[at(pos), sum_cut(k)] + running[at(pos), sum_cut(k)]
+
+                @pl.when((pos > deep) & (deep < inner))
                 def _():
-                    go_up(d, k).start()
-
-            @pl.when(t >= LINE - 1 - u)
-            def _():
-                d = t - (LINE - 1) + u
-
-                @pl.when(u < LINE - 1)
+                    inward(pos, k).start()
+
+                @pl.when((pos > deep) & (deep == inner))
                 def _():
-                    go_down(d, k).wait_recv()
-                    sums[d, cut] = sums[d, cut] + from_high[d, cut]
-
-                @pl.when(d < u)
-                def _():
-                    go_down(d, k).start()
+                    across(pos, k).start()
 
         return 0
 
     lax.fori_loop(0, LINE, reduce_step, 0)
+    for pos in range(1, HALF):
+
+        @pl.when(pos > deep)
+        def _():
+            term_arrival(pos).wait_recv()
+            sums[u] = sums[u] + terms[pos]
+
+    for k in range(len(SUM_CUTS)):
+        across(inner + 1, k).wait_recv()
 
     def to_half(k):
         ref = routed[k].at[x, h]
@@ -323,11 +357,40 @@
 
     cuts = range(len(CUTS))
     for k, (a, m) in enumerate(CUTS):
-        piece = jax.nn.gelu(sums[u, a : a + m], approximate=True).astype(jnp.bfloat16)
+        piece = sums[u, a : a + m] + crossed[a : a + m]
+        piece = jax.nn.gelu(piece, approximate=True).astype(jnp.bfloat16)
         routed[k][x, h] = piece
         to_half(k).start()
         for i in range(1, n_x):
             x_copy(i, h, k).start()
+    start_exchange(sf_send, sf_recv, sf_sems)
+
+    seq = 2 * LINE * tok
+    contract_last = (((1,), (1,)), ((), ()))
+    chunk = LANES
+    per = chunk // tok
+    zero = jnp.zeros((), jnp.bfloat16)
+    head_of = lax.broadcasted_iota(jnp.int32, (tok, width), 1) // HD
+
+    def apart(rows):
+        return jnp.concatenate([jnp.where(head_of == n, rows, zero) for n in range(HEADS)], axis=0)
+
+    fresh_scores = lax.dot_general(
+        apart(image_q_ref[0]), fresh_ref[0, :, :width], contract_last, preferred_element_type=jnp.float32
+    )
+    fresh_scores = fresh_scores * HD ** (-0.5)
+    fresh_base = jnp.max(fresh_scores, axis=-1, keepdims=True)
+    fresh_weights = jnp.exp(fresh_scores - fresh_base)
+    fresh_total = jnp.sum(fresh_weights, axis=-1, keepdims=True)
+    fresh_weights = fresh_weights.astype(jnp.bfloat16)
+    fresh_stats[:, 0:1] = fresh_base
+    fresh_stats[:, 1:2] = fresh_total
+    fresh_blend[...] = jnp.dot(
+        jnp.concatenate([fresh_weights[n * tok : (n + 1) * tok] for n in range(HEADS)], axis=1),
+        apart(fresh_ref[0, :, width:]),
+        preferred_element_type=jnp.float32,
+    )
+
     for k in cuts:
         half_arrival(k).wait_recv()
         for i in range(1, n_x):
@@ -350,48 +413,33 @@
         to_other_core(c, here, k).start()
 
     end_exchange(sf_send, sf_recv, sf_sems)
-    seq = 2 * LINE * tok
-    whole = sf_recv[...].reshape(seq, 3 * LANES)
+    whole = sf_recv[...].reshape(seq, 2 * LANES)
     queries, keys, values = whole[:, :HD], whole[:, HD : 2 * HD], whole[:, 2 * HD : 3 * HD]
-    new_keys, new_values = whole[:, 3 * HD : 4 * HD], whole[:, 4 * HD : 5 * HD]
-    contract_last = (((1,), (1,)), ((), ()))
-    chunk = LANES
     own = (
         lax.broadcasted_iota(jnp.int32, (chunk, chunk), 0) // tok
         == lax.broadcasted_iota(jnp.int32, (chunk, chunk), 1) // tok
     )
-    zero = jnp.zeros((), jnp.bfloat16)
-
-    def blended(scores, head_values):
-        weights = jnp.exp(scores - jnp.max(scores, axis=-1, keepdims=True))
-        return weights, jnp.sum(weights, axis=-1, keepdims=True)
-
-    out_pad = jnp.zeros((chunk, LANES - HD), jnp.bfloat16)
-    per = chunk // tok
+    self_pad = jnp.zeros((chunk, LANES - HD - 3), jnp.bfloat16)
     for i in range(seq // chunk):
         a, b = i * chunk, (i + 1) * chunk
         scores = lax.dot_general(queries[a:b], keys, contract_last, preferred_element_type=jnp.float32)
-        mine = lax.dot_general(queries[a:b], new_keys[a:b], contract_last, preferred_element_type=jnp.float32)
-        mixed = [jnp.where(own, mine, scores[:, a:b])]
+        scores = scores * HD ** (-0.5)
+        mixed = [jnp.where(own, masked_score, scores[:, a:b])]
         if a > 0:
             mixed = [scores[:, :a]] + mixed
         if b < seq:
             mixed = mixed + [scores[:, b:]]
-        scores = jnp.concatenate(mixed, axis=1) * HD ** (-0.5)
-        weights, total = blended(scores, values)
-        weights = weights.astype(jnp.bfloat16)
-        near = weights[:, a:b]
-        mixed = [jnp.where(own, zero, near)]
-        if a > 0:
-            mixed = [weights[:, :a]] + mixed
-        if b < seq:
-            mixed = mixed + [weights[:, b:]]
-        result = jnp.dot(jnp.concatenate(mixed, axis=1), values, preferred_element_type=jnp.float32)
-        result = result + jnp.dot(
-            jnp.where(own, near, zero), new_values[a:b], preferred_element_type=jnp.float32
-        )
+        scores = jnp.concatenate(mixed, axis=1)
+        base = jnp.max(scores, axis=-1, keepdims=True).astype(jnp.bfloat16)
+        weights = jnp.exp(scores - base.astype(jnp.float32))
+        total = jnp.sum(weights, axis=-1, keepdims=True)
+        result = jnp.dot(weights.astype(jnp.bfloat16), values, preferred_element_type=jnp.float32)
         result = (result / total).astype(jnp.bfloat16)
-        so_send[i * per : (i + 1) * per] = jnp.concatenate([result, out_pad], axis=1).reshape(per, tok, LANES)
+        total_high = total.astype(jnp.bfloat16)
+        total_low = (total - total_high.astype(jnp.float32)).astype(jnp.bfloat16)
+        so_send[i * per : (i + 1) * per] = jnp.concatenate(
+            [result, base, total_high, total_low, self_pad], axis=1
+        ).reshape(per, tok, LANES)
     start_exchange(so_send, so_recv, so_sems)
 
     for k in cuts:
@@ -421,6 +469,7 @@
         caption_rows, kv_w_ref[...], contract_last, preferred_element_type=jnp.float32
     ).astype(jnp.bfloat16)
     prompt_keys, prompt_values = head_states[:, :HD], head_states[:, HD : 2 * HD]
+    out_pad = jnp.zeros((chunk, LANES - HD), jnp.bfloat16)
     length = lengths_ref[source]
     visible = lax.broadcasted_iota(jnp.int32, (1, row_tiles * TILE), 1) < length
     cross_rows = cq_recv[...].reshape(seq, LANES)[:, :HD]
@@ -428,31 +477,52 @@
         a, b = i * chunk, (i + 1) * chunk
         scores = lax.dot_general(cross_rows[a:b], prompt_keys, contract_last, preferred_element_type=jnp.float32)
         scores = jnp.where(visible, scores * HD ** (-0.5), masked_score)
-        weights, total = blended(scores, prompt_values)
+        weights = jnp.exp(scores - jnp.max(scores, axis=-1, keepdims=True))
+        total = jnp.sum(weights, axis=-1, keepdims=True)
         result = jnp.dot(weights.astype(jnp.bfloat16), prompt_values, preferred_element_type=jnp.float32)
         result = (result / total).astype(jnp.bfloat16)
         co_send[i * per : (i + 1) * per] = jnp.concatenate([result, out_pad], axis=1).reshape(per, tok, LANES)
     start_exchange(co_send, co_recv, co_sems)
 
     end_exchange(so_send, so_recv, so_sems)
-    self_out_ref[0] = jnp.concatenate([so_recv[n][:, :HD].astype(jnp.float32) for n in range(HEADS)], axis=1)
+    merged = []
+    for n in range(HEADS):
+        block = so_recv[n].astype(jnp.float32)
+        stale_base = block[:, HD : HD + 1]
+        stale_total = block[:, HD + 1 : HD + 2] + block[:, HD + 2 : HD + 3]
+        own_base = fresh_stats[n * tok : (n + 1) * tok, 0:1]
+        own_total = fresh_stats[n * tok : (n + 1) * tok, 1:2]
+        top = jnp.maximum(stale_base, own_base)
+        stale_share = stale_total * jnp.exp(stale_base - top)
+        own_scale = jnp.exp(own_base - top)
+        both = stale_share + own_total * own_scale
+        merged.append(
+            block[:, :HD] * (stale_share / both) + fresh_blend[:, n * HD : (n + 1) * HD] * (own_scale / both)
+        )
+    self_out_ref[0] = jnp.concatenate(merged, axis=1)
     end_exchange(co_send, co_recv, co_sems)
     cross_out_ref[0] = jnp.concatenate([co_recv[n][:, :HD].astype(jnp.float32) for n in range(HEADS)], axis=1)
 
-    for k in range(len(SUM_CUTS)):
-
-        def drain(q, _):
-            @pl.when(q > u)
+    for pos in range(inner):
+
+        @pl.when(pos < deep)
+        def _():
+            outward(pos).wait_send()
+
+    def drain(pos, _):
+        for k in range(len(SUM_CUTS)):
+
+            @pl.when((pos > deep) & (deep < inner))
             def _():
-                go_up(q, k).wait_send()
-
-            @pl.when(q < u)
+                inward(pos, k).wait_send()
+
+            @pl.when((pos > deep) & (deep == inner))
             def _():
-                go_down(q, k).wait_send()
-
-            return 0
-
-        lax.fori_loop(0, LINE, drain, 0)
+                across(pos, k).wait_send()
+
+        return 0
+
+    lax.fori_loop(0, LINE, drain, 0)
     for k in cuts:
         to_half(k).wait_send()
         for i in range(1, n_x):
@@ -507,7 +577,7 @@
     sum_lines, lines, cuts = (LINE, len(SUM_CUTS)), (LINE, len(CUTS)), len(CUTS)
     hbm = pl.BlockSpec(memory_space=pltpu.HBM)
     by_head = pltpu.VMEM((HEADS, tok, LANES), bf16)
-    by_head_wide = pltpu.VMEM((HEADS, tok, 3 * LANES), bf16)
+    by_head_wide = pltpu.VMEM((HEADS, tok, 2 * LANES), bf16)
     return pl.pallas_call(
         functools.partial(kernel, dims),
         out_shape=[jax.ShapeDtypeStruct((1, tok, width), f32)] * 2,
@@ -518,7 +588,8 @@
             pltpu.VMEM((2, LINE, *piece), f32),
             pltpu.VMEM((LINE, *piece), f32),
             pltpu.VMEM((LINE, *piece), f32),
-            pltpu.VMEM((LINE, *piece), f32),
+            pltpu.VMEM(piece, f32),
+            pltpu.VMEM((HALF, *piece), f32),
             [pltpu.VMEM((n_x, n_h, m, TILE, LANES), bf16) for _, m in CUTS],
             [pltpu.VMEM((n_y, m, TILE, LANES), bf16) for _, m in CUTS],
             [pltpu.VMEM((n_y, m, TILE, LANES), bf16) for _, m in CUTS],
@@ -531,10 +602,13 @@
             by_head,
             by_head,
             by_head,
+            pltpu.VMEM((HEADS * tok, LANES), f32),
+            pltpu.VMEM((tok, width), f32),
             dma((len(operands),)),
             dma((2,)),
             dma((2, *sum_lines)),
             dma((2, *sum_lines)),
+            dma((2, HALF)),
             dma((2, cuts)),
             dma((2, cuts, n_h, n_x)),
             dma((2, cuts, n_y)),
@@ -547,7 +621,7 @@
             dma((2, HEADS)),
         ],
         compiler_params=pltpu.CompilerParams(
-            collective_id=0, has_side_effects=True, vmem_limit_bytes=60 * 1024 * 1024
+            collective_id=0, has_side_effects=True, vmem_limit_bytes=56 * 1024 * 1024
         ),
     )(prompt_route, prompt_lengths, *operands)
 

time: 97.9 us -> 85.2 us (0.87)
  Pallas kernels: 94.8 us -> 82.1 us
    pallas_call x1, Pallas kernels: 94.8 us -> 82.1 us  [shards(): pl.pallas_call(functools.partial(kernel, dims), out_shape=[jax.ShapeDtype...]
where the time goes in v3:
time: 85.2 us; the launch traced here: 85.1 us
  Pallas kernels  82.1 us (96%)
  local copies, waits for them, and re-layouts  2.28 us (3%)
    pallas_call x1, Pallas kernels, shards(): pl.pallas_call(functools.partial(kernel, dims), out_shape=[jax.ShapeDtype...  82.1 us
    unnamed x4, local copies, waits for them, and re-layouts  2.28 us

profile of v3, /device:TPU:1, one launch (start us, length us, event | category | flops | bytes accessed | tf_op | source)
XLA Modules:
  0.0 85.1 jit_solution(6814061891967703615)
XLA Ops:
  0.6 82.1 %shard_map.104 = (f32[1,32,1152]{2,1,0:T(8,128)}, f32[1,32,1152]{2,1,0:T(8,128)}) custom-call(s32[32]{0:T(128)} %route_ref.1, s32[32]{0:T(128)} %lengths_ref.1, bf16[1,300,256]{2,1,0:T(8,128)(2,1)} %prompt_hbm.1, bf16[256,1152]{1,0:T(8,128)(2,1)} %caption_w_hbm.1, bf16[144,1152]{1,0:T(8,128)(2,1)} %bitcast.1, bf16[1,32,1152]{2,1,0:T(8,128)(2,1)} %image_q_hbm.1, ...), custom_call_target="tpu_custom_call" | custom-call | tf_op jit(solution)/shard_map/pallas_call | solution.py:581
  82.8 0.0 copy-start
  82.8 1.6 %copy.13 = f32[1,32,1152]{2,1,0:T(8,128)} copy(f32[1,32,1152]{2,1,0:T(8,128)} %get-tuple-element.4) | data formatting | bytes 294912
  84.4 0.0 copy-done
  84.4 0.7 copy.14
Async XLA Ops:
  82.8 1.6 %copy-start = (f32[1,32,1152]{2,1,0:T(8,128)S(1)}, f32[1,32,1152]{2,1,0:T(8,128)}, u32[]{:S(2)}) copy-start(f32[1,32,1152]{2,1,0:T(8,128)} %get-tuple-element.5) | copy-start | bytes 442372

commit v4 on v3

--- a/solution.py
+++ b/solution.py
@@ -14,10 +14,10 @@
 TILES = 11
 LINE = 8
 HALF = LINE // 2
+masked_score = -1e30
+MESH = pl.DeviceIdType.MESH
 SUM_CUTS = ((0, 3), (3, 3), (6, 3), (9, 2))
 CUTS = ((0, 6), (6, 5))
-masked_score = -1e30
-MESH = pl.DeviceIdType.MESH
 
 
 def kernel(
@@ -162,9 +162,18 @@
     for t in range(row_tiles * col_tiles, 2 * LINE * TILES):
         part[t // (LINE * TILES), slots[(t // TILES) % LINE], t % TILES] = jnp.zeros((TILE, LANES), jnp.float32)
 
-    to_twin = copy(part.at[1 - c], sib_part, sib_sems.at[0], sib_sems.at[1], twin)
+    left = u < HALF
+    deep = jnp.where(left, u, LINE - 1 - u)
+
+    def at(pos):
+        return jnp.where(left, pos, LINE - 1 - pos)
+
+    def to_twin(pos):
+        return copy(part.at[1 - c, at(pos)], sib_part.at[at(pos)], sib_sems.at[0, pos], sib_sems.at[1, pos], twin)
+
     pl.semaphore_wait(barrier, greeted)
-    to_twin.start()
+    for pos in reversed(range(LINE)):
+        to_twin(pos).start()
     for load in loads[2:]:
         load.wait()
 
@@ -201,6 +210,20 @@
 
         lax.fori_loop(1, 2 * LINE, step, 0)
 
+    def start_some(send, recv, sems, first, count):
+        def step(n, _):
+            @pl.when(n == me_p)
+            def _():
+                recv[n] = send[n]
+
+            @pl.when(n != me_p)
+            def _():
+                exchange(send, recv, sems, (n - me_p + 2 * LINE) % (2 * LINE)).start()
+
+            return 0
+
+        lax.fori_loop(first, first + count, step, 0)
+
     def end_exchange(send, recv, sems):
         def step(i, _):
             arrival(send, recv, sems, i).wait_recv()
@@ -216,23 +239,13 @@
         lax.fori_loop(1, 2 * LINE, step, 0)
 
     start_exchange(cq_send, cq_recv, cq_sems)
-    to_twin.wait_recv()
-    to_twin.wait_send()
     sums = part.at[c]
 
-    def add_twin(i, _):
-        sums[i] = sums[i] + sib_part[i]
-        return 0
-
-    lax.fori_loop(0, LINE, add_twin, 0)
+    def add_twin(pos):
+        to_twin(pos).wait_recv()
+        sums[at(pos)] = sums[at(pos)] + sib_part[at(pos)]
 
     inner = HALF - 1
-    left = u < HALF
-    deep = jnp.where(left, u, LINE - 1 - u)
-
-    def at(pos):
-        return jnp.where(left, pos, LINE - 1 - pos)
-
     def at_device(pos):
         return {"patch": 2 * at(pos) + c}
 
@@ -266,14 +279,26 @@
     def term_arrival(pos):
         return copy(sums.at[u], terms.at[pos], term_sems.at[0, 0], term_sems.at[1, pos], at_device(pos))
 
-    for pos in range(inner):
+    def first_step(t, _):
+        pos = LINE - 1 - t
+        add_twin(pos)
 
         @pl.when(pos < deep)
         def _():
             outward(pos).start()
 
+        return 0
+
+    @pl.when(deep > 0)
+    def _():
+        lax.fori_loop(0, LINE, first_step, 0)
+
     def reduce_step(t, _):
         pos = LINE - 1 - t
+
+        @pl.when(deep == 0)
+        def _():
+            add_twin(pos)
 
         @pl.when(pos >= deep)
         def _():
@@ -363,8 +388,6 @@
         to_half(k).start()
         for i in range(1, n_x):
             x_copy(i, h, k).start()
-    start_exchange(sf_send, sf_recv, sf_sems)
-
     seq = 2 * LINE * tok
     contract_last = (((1,), (1,)), ((), ()))
     chunk = LANES
@@ -395,6 +418,7 @@
         half_arrival(k).wait_recv()
         for i in range(1, n_x):
             x_copy(i, 1 - h, k).start()
+    start_exchange(sf_send, sf_recv, sf_sems)
     for k in cuts:
         for i in range(1, n_x):
             x_arrival(i, h, k).wait_recv()
@@ -412,6 +436,11 @@
             spread(here, i, i, k).start()
         to_other_core(c, here, k).start()
 
+    for k in cuts:
+        gathered(there, k).wait_recv()
+        for i in range(1, HALF):
+            spread(there, i, HALF - 1 + i, k).start()
+        to_other_core(c, there, k).start()
     end_exchange(sf_send, sf_recv, sf_sems)
     whole = sf_recv[...].reshape(seq, 2 * LANES)
     queries, keys, values = whole[:, :HD], whole[:, HD : 2 * HD], whole[:, 2 * HD : 3 * HD]
@@ -440,13 +469,8 @@
         so_send[i * per : (i + 1) * per] = jnp.concatenate(
             [result, base, total_high, total_low, self_pad], axis=1
         ).reshape(per, tok, LANES)
-    start_exchange(so_send, so_recv, so_sems)
-
-    for k in cuts:
-        gathered(there, k).wait_recv()
-        for i in range(1, HALF):
-            spread(there, i, HALF - 1 + i, k).start()
-        to_other_core(c, there, k).start()
+        start_some(so_send, so_recv, so_sems, i * per, per)
+
     for far in (0, HALF):
         for k in cuts:
             for i in range(1, HALF):
@@ -482,7 +506,7 @@
         result = jnp.dot(weights.astype(jnp.bfloat16), prompt_values, preferred_element_type=jnp.float32)
         result = (result / total).astype(jnp.bfloat16)
         co_send[i * per : (i + 1) * per] = jnp.concatenate([result, out_pad], axis=1).reshape(per, tok, LANES)
-    start_exchange(co_send, co_recv, co_sems)
+        start_some(co_send, co_recv, co_sems, i * per, per)
 
     end_exchange(so_send, so_recv, so_sems)
     merged = []
@@ -500,9 +524,6 @@
             block[:, :HD] * (stale_share / both) + fresh_blend[:, n * HD : (n + 1) * HD] * (own_scale / both)
         )
     self_out_ref[0] = jnp.concatenate(merged, axis=1)
-    end_exchange(co_send, co_recv, co_sems)
-    cross_out_ref[0] = jnp.concatenate([co_recv[n][:, :HD].astype(jnp.float32) for n in range(HEADS)], axis=1)
-
     for pos in range(inner):
 
         @pl.when(pos < deep)
@@ -523,6 +544,8 @@
         return 0
 
     lax.fori_loop(0, LINE, drain, 0)
+    for pos in range(LINE):
+        to_twin(pos).wait_send()
     for k in cuts:
         to_half(k).wait_send()
         for i in range(1, n_x):
@@ -543,6 +566,9 @@
     drain_exchange(cq_send, cq_recv, cq_sems)
     drain_exchange(sf_send, sf_recv, sf_sems)
     drain_exchange(so_send, so_recv, so_sems)
+    end_exchange(co_send, co_recv, co_sems)
+    cross_out_ref[0] = jnp.concatenate([co_recv[n][:, :HD].astype(jnp.float32) for n in range(HEADS)], axis=1)
+
     drain_exchange(co_send, co_recv, co_sems)
 
 
@@ -580,7 +606,7 @@
     by_head_wide = pltpu.VMEM((HEADS, tok, 2 * LANES), bf16)
     return pl.pallas_call(
         functools.partial(kernel, dims),
-        out_shape=[jax.ShapeDtypeStruct((1, tok, width), f32)] * 2,
+        out_shape=[pltpu.VMEM((1, tok, width), f32)] * 2,
         in_specs=[smem, smem] + [hbm] * 7,
         out_specs=[vmem, vmem],
         scratch_shapes=[
@@ -605,7 +631,7 @@
             pltpu.VMEM((HEADS * tok, LANES), f32),
             pltpu.VMEM((tok, width), f32),
             dma((len(operands),)),
-            dma((2,)),
+            dma((2, LINE)),
             dma((2, *sum_lines)),
             dma((2, *sum_lines)),
             dma((2, HALF)),
@@ -621,9 +647,9 @@
             dma((2, HEADS)),
         ],
         compiler_params=pltpu.CompilerParams(
-            collective_id=0, has_side_effects=True, vmem_limit_bytes=56 * 1024 * 1024
+            collective_id=0, has_side_effects=True, vmem_limit_bytes=48 * 1024 * 1024
         ),
-    )(prompt_route, prompt_lengths, *operands)
+    )(prompt_route, prompt_lengths, *(pltpu.with_memory_space_constraint(a, pltpu.HBM) for a in operands))
 
 
 def solution(mesh, dims=(4, 2, 4)):

time: 85.2 us -> 80.8 us (0.948)
  Pallas kernels: 82.1 us -> 78 us
    pallas_call x1, Pallas kernels: 82.1 us -> 78 us  [shards(): pl.pallas_call(functools.partial(kernel, dims), out_shape=[pltpu.VMEM((1,...]
    unnamed x4 -> x6, local copies, waits for them, and re-layouts: 2.28 us -> 1.98 us
where the time goes in v4:
time: 80.8 us; the launch traced here: 80.7 us
  Pallas kernels  78 us (97%)
  local copies, waits for them, and re-layouts  1.98 us (2%)
    pallas_call x1, Pallas kernels, shards(): pl.pallas_call(functools.partial(kernel, dims), out_shape=[pltpu.VMEM((1,...  78 us
    unnamed x6, local copies, waits for them, and re-layouts  1.98 us

profile of v4, /device:TPU:1, one launch (start us, length us, event | category | flops | bytes accessed | tf_op | source)
XLA Modules:
  0.0 80.7 jit_solution(8002803610688952958)
XLA Ops:
  0.6 0.0 copy-start
  0.6 0.0 copy-start.1
  0.7 0.6 copy-done
  1.3 0.0 copy-done.1
  1.3 78.0 %shard_map.104 = (f32[1,32,1152]{2,1,0:T(8,128)S(1)}, f32[1,32,1152]{2,1,0:T(8,128)S(1)}) custom-call(s32[32]{0:T(128)S(1)} %copy-done, s32[32]{0:T(128)S(1)} %copy-done.1, bf16[1,300,256]{2,1,0:T(8,128)(2,1)} %prompt_hbm.1, bf16[256,1152]{1,0:T(8,128)(2,1)} %caption_w_hbm.1, bf16[144,1152]{1,0:T(8,128)(2,1)} %bitcast.1, bf16[1,32,1152]{2,1,0:T(8,128)(2,1)} %image_q_hbm.1, ...), custom_call_target="tpu_custom_call" | custom-call | tf_op jit(solution)/shard_map/pallas_call | solution.py:607
  79.3 0.7 copy.13
  80.0 0.7 copy.14
Async XLA Ops:
  0.6 0.7 copy-start
  0.6 0.7 copy-start.1

commit v5 on v4

--- a/solution.py
+++ b/solution.py
@@ -18,6 +18,10 @@
 MESH = pl.DeviceIdType.MESH
 SUM_CUTS = ((0, 3), (3, 3), (6, 3), (9, 2))
 CUTS = ((0, 6), (6, 5))
+
+
+def far_first(size):
+    return sorted(range(1, size), key=lambda i: -min(i, size - i))
 
 
 def kernel(
@@ -386,7 +390,7 @@
         piece = jax.nn.gelu(piece, approximate=True).astype(jnp.bfloat16)
         routed[k][x, h] = piece
         to_half(k).start()
-        for i in range(1, n_x):
+        for i in far_first(n_x):
             x_copy(i, h, k).start()
     seq = 2 * LINE * tok
     contract_last = (((1,), (1,)), ((), ()))
@@ -416,14 +420,14 @@
 
     for k in cuts:
         half_arrival(k).wait_recv()
-        for i in range(1, n_x):
+        for i in far_first(n_x):
             x_copy(i, 1 - h, k).start()
     start_exchange(sf_send, sf_recv, sf_sems)
     for k in cuts:
         for i in range(1, n_x):
             x_arrival(i, h, k).wait_recv()
             x_arrival(i, 1 - h, k).wait_recv()
-        for i in range(1, n_y):
+        for i in far_first(n_y):
             y_send[k][i] = wanted(i, k)
             y_copy(i, k).start()
         y_recv[k][y] = wanted(0, k)
@@ -432,7 +436,9 @@
         for i in range(1, n_y):
             y_arrival(i, k).wait_recv()
         caption[c, here, a : a + m] = y_recv[k][lax.div(source, n_h * n_x)]
-        for i in range(HALF):
+        spread(here, 0, 0, k).start()
+    for k in cuts:
+        for i in range(1, HALF):
             spread(here, i, i, k).start()
         to_other_core(c, here, k).start()
 

time: 80.8 us -> 79.5 us (0.984)
  Pallas kernels: 78 us -> 76.7 us
    pallas_call x1, Pallas kernels: 78 us -> 76.7 us  [shards(): pl.pallas_call(functools.partial(kernel, dims), out_shape=[pltpu.VMEM((1,...]
where the time goes in v5:
time: 79.5 us; the launch traced here: 79.3 us
  Pallas kernels  76.7 us (96%)
  local copies, waits for them, and re-layouts  1.98 us (2%)
    pallas_call x1, Pallas kernels, shards(): pl.pallas_call(functools.partial(kernel, dims), out_shape=[pltpu.VMEM((1,...  76.7 us
    unnamed x6, local copies, waits for them, and re-layouts  1.98 us

profile of v5, /device:TPU:1, one launch (start us, length us, event | category | flops | bytes accessed | tf_op | source)
XLA Modules:
  0.0 79.3 jit_solution(15360868514906722267)
XLA Ops:
  0.6 0.0 copy-start
  0.6 0.0 copy-start.1
  0.7 0.6 copy-done
  1.3 0.0 copy-done.1
  1.3 76.7 %shard_map.104 = (f32[1,32,1152]{2,1,0:T(8,128)S(1)}, f32[1,32,1152]{2,1,0:T(8,128)S(1)}) custom-call(s32[32]{0:T(128)S(1)} %copy-done, s32[32]{0:T(128)S(1)} %copy-done.1, bf16[1,300,256]{2,1,0:T(8,128)(2,1)} %prompt_hbm.1, bf16[256,1152]{1,0:T(8,128)(2,1)} %caption_w_hbm.1, bf16[144,1152]{1,0:T(8,128)(2,1)} %bitcast.1, bf16[1,32,1152]{2,1,0:T(8,128)(2,1)} %image_q_hbm.1, ...), custom_call_target="tpu_custom_call" | custom-call | tf_op jit(solution)/shard_map/pallas_call | solution.py:613
  78.0 0.7 copy.13
  78.7 0.7 copy.14
Async XLA Ops:
  0.6 0.7 copy-start
  0.6 0.7 copy-start.1

commit v6 on v5

--- a/solution.py
+++ b/solution.py
@@ -35,8 +35,7 @@
     cross_q_hbm,
     fresh_hbm,
     stale_hbm,
-    self_out_ref,
-    cross_out_ref,
+    out_ref,
     prompt_ref,
     caption_w_ref,
     kv_w_ref,
@@ -529,7 +528,7 @@
         merged.append(
             block[:, :HD] * (stale_share / both) + fresh_blend[:, n * HD : (n + 1) * HD] * (own_scale / both)
         )
-    self_out_ref[0] = jnp.concatenate(merged, axis=1)
+    out_ref[0] = jnp.concatenate(merged, axis=1)
     for pos in range(inner):
 
         @pl.when(pos < deep)
@@ -573,7 +572,7 @@
     drain_exchange(sf_send, sf_recv, sf_sems)
     drain_exchange(so_send, so_recv, so_sems)
     end_exchange(co_send, co_recv, co_sems)
-    cross_out_ref[0] = jnp.concatenate([co_recv[n][:, :HD].astype(jnp.float32) for n in range(HEADS)], axis=1)
+    out_ref[1] = jnp.concatenate([co_recv[n][:, :HD].astype(jnp.float32) for n in range(HEADS)], axis=1)
 
     drain_exchange(co_send, co_recv, co_sems)
 
@@ -610,11 +609,11 @@
     hbm = pl.BlockSpec(memory_space=pltpu.HBM)
     by_head = pltpu.VMEM((HEADS, tok, LANES), bf16)
     by_head_wide = pltpu.VMEM((HEADS, tok, 2 * LANES), bf16)
-    return pl.pallas_call(
+    both = pl.pallas_call(
         functools.partial(kernel, dims),
-        out_shape=[pltpu.VMEM((1, tok, width), f32)] * 2,
+        out_shape=pltpu.VMEM((2, tok, width), f32),
         in_specs=[smem, smem] + [hbm] * 7,
-        out_specs=[vmem, vmem],
+        out_specs=vmem,
         scratch_shapes=[
             *(pltpu.VMEM(array.shape, bf16) for array in operands),
             pltpu.VMEM((2, LINE, *piece), f32),
@@ -656,6 +655,7 @@
             collective_id=0, has_side_effects=True, vmem_limit_bytes=48 * 1024 * 1024
         ),
     )(prompt_route, prompt_lengths, *(pltpu.with_memory_space_constraint(a, pltpu.HBM) for a in operands))
+    return both[0:1], both[1:2]
 
 
 def solution(mesh, dims=(4, 2, 4)):

time: 79.5 us -> 78.9 us (level)
    unnamed x6 -> x4, local copies, waits for them, and re-layouts: 1.98 us -> 0.66 us
where the time goes in v6:
time: 78.9 us; the launch traced here: 78.7 us
  Pallas kernels  76.7 us (97%)
  local copies, waits for them, and re-layouts  1.39 us (2%)
    pallas_call x1, Pallas kernels, shards(): pl.pallas_call(functools.partial(kernel, dims), out_shape=pltpu.VMEM((2,...  76.7 us

profile of v6, /device:TPU:1, one launch (start us, length us, event | category | flops | bytes accessed | tf_op | source)
XLA Modules:
  0.0 78.7 jit_solution(4296910418828420339)
XLA Ops:
  0.6 0.0 copy-start
  0.6 0.0 copy-start.1
  0.7 0.6 copy-done
  1.3 0.0 copy-done.1
  1.3 76.7 %shard_map.104 = f32[2,32,1152]{2,1,0:T(8,128)S(1)} custom-call(s32[32]{0:T(128)S(1)} %copy-done, s32[32]{0:T(128)S(1)} %copy-done.1, bf16[1,300,256]{2,1,0:T(8,128)(2,1)} %prompt_hbm.1, bf16[256,1152]{1,0:T(8,128)(2,1)} %caption_w_hbm.1, bf16[144,1152]{1,0:T(8,128)(2,1)} %bitcast.1, bf16[1,32,1152]{2,1,0:T(8,128)(2,1)} %image_q_hbm.1, ...), custom_call_target="tpu_custom_call" | custom-call | tf_op jit(solution)/shard_map/pallas_call | solution.py:612
  78.0 0.7 fusion
Async XLA Ops:
  0.6 0.7 copy-start
  0.6 0.7 copy-start.1

commit v7 on v6

--- a/solution.py
+++ b/solution.py
@@ -211,7 +211,9 @@
             exchange(send, recv, sems, i).start()
             return 0
 
-        lax.fori_loop(1, 2 * LINE, step, 0)
+        lax.fori_loop(5, 12, step, 0)
+        lax.fori_loop(1, 5, step, 0)
+        lax.fori_loop(12, 2 * LINE, step, 0)
 
     def start_some(send, recv, sems, first, count):
         def step(n, _):

time: 78.9 us -> 80.2 us (1.016)
  Pallas kernels: 76.7 us -> 78 us
    pallas_call x1, Pallas kernels: 76.7 us -> 78 us  [shards(): pl.pallas_call(functools.partial(kernel, dims), out_shape=pltpu.VMEM((2,...]
where the time goes in v7:
time: 80.2 us; the launch traced here: 80.1 us
  Pallas kernels  78 us (97%)
  local copies, waits for them, and re-layouts  1.39 us (2%)
    pallas_call x1, Pallas kernels, shards(): pl.pallas_call(functools.partial(kernel, dims), out_shape=pltpu.VMEM((2,...  78 us

profile of v7, /device:TPU:1, one launch (start us, length us, event | category | flops | bytes accessed | tf_op | source)
XLA Modules:
  0.0 80.1 jit_solution(6997924445865916178)
XLA Ops:
  0.6 0.0 copy-start
  0.6 0.0 copy-start.1
  0.7 0.6 copy-done
  1.3 0.0 copy-done.1
  1.3 78.0 %shard_map.104 = f32[2,32,1152]{2,1,0:T(8,128)S(1)} custom-call(s32[32]{0:T(128)S(1)} %copy-done, s32[32]{0:T(128)S(1)} %copy-done.1, bf16[1,300,256]{2,1,0:T(8,128)(2,1)} %prompt_hbm.1, bf16[256,1152]{1,0:T(8,128)(2,1)} %caption_w_hbm.1, bf16[144,1152]{1,0:T(8,128)(2,1)} %bitcast.1, bf16[1,32,1152]{2,1,0:T(8,128)(2,1)} %image_q_hbm.1, ...), custom_call_target="tpu_custom_call" | custom-call | tf_op jit(solution)/shard_map/pallas_call | solution.py:614
  79.3 0.7 fusion
Async XLA Ops:
  0.6 0.7 copy-start
  0.6 0.7 copy-start.1
